TPU v7x, 32 devices: a whole 2x2x4 slice. The times are simulated.
32 devices in a mesh: section: 8 (over y, x, core), tensor: 4 (over z).
Axes of the slice: x: 2, y: 2, z: 4, core: 2. Of those that a mesh axis runs over, the one named last changes fastest.
Arguments:
- inflow: bfloat16 [8, 512, 12288], P('section', 'tensor'), may hold values from -60 to 60
- fresh: bfloat16 [512, 12288], P('tensor'), may hold values from -60 to 60
- stash_held: bfloat16 [8, 512, 12288], P('section', 'tensor'), may hold values from -60 to 60
- grad_in: bfloat16 [8, 512, 12288], P('section', 'tensor'), may hold values from -6 to 6
- query_gain: float32 [8, 12288], P('section', 'tensor'), may hold values from -3 to 3
- key_gain: float32 [8, 12288], P('section', 'tensor'), may hold values from -3 to 3
- value_gain: float32 [8, 12288], P('section', 'tensor'), may hold values from -4 to 4
Outputs:
- first_out: bfloat16 [8, 512, 12288], P('section', 'tensor')
- second_out: bfloat16 [8, 512, 12288], P('section', 'tensor')
- evicted: bfloat16 [8, 512, 12288], P('section', 'tensor')
- grad_out: bfloat16 [8, 512, 12288], P('section', 'tensor')
All inputs are finite; a program needn't handle non-finite values.
Results may differ from a plain program's by a relative error of at most 0.0068.
Values may be sent and summed in bfloat16 or wider, within the bound.
A program may use at most 192 MiB of HBM per device.

v0:
```python
import jax
import jax.numpy as jnp
from jax import lax
from jax.sharding import PartitionSpec as P

HDIM = 128


epsilon = 1e-05
masked_score = -1e30


def from_partner(value, axis, distance):
    mask = 2**distance
    pairs = [(source, source ^ mask) for source in range(lax.axis_size(axis))]
    return lax.ppermute(value, axis, pairs)


def from_behind(x, axis, by):
    peers = lax.axis_size(axis)
    pairs = [(i, i + by) for i in range(peers) if 0 <= i + by < peers]
    return lax.ppermute(x, axis, pairs)


def normalize(tokens_in):
    values = tokens_in.astype(jnp.float32)
    factor = lax.rsqrt(jnp.mean(values * values, axis=-1, keepdims=True) + epsilon)
    return (values * factor, factor)


def heads_of(normed, feature_gain):
    scaled = (normed.astype(jnp.float32) * feature_gain).astype(jnp.bfloat16)
    return scaled.reshape(scaled.shape[0], -1, HDIM)


def softmax_causal(queries, key_heads):
    scores = jnp.einsum("ihd,jhd->hij", queries, key_heads, preferred_element_type=jnp.float32)
    scores = scores * HDIM ** (-0.5)
    length = queries.shape[0]
    row_index = lax.broadcasted_iota(jnp.int32, (length, length), 0)
    col_index = lax.broadcasted_iota(jnp.int32, (length, length), 1)
    scores = jnp.where(row_index >= col_index, scores, masked_score)
    largest = jnp.max(scores, axis=-1, keepdims=True)
    weights = jnp.exp(scores - largest)
    return weights / jnp.sum(weights, axis=-1, keepdims=True)


def forward(tokens_in, query_gain, key_gain, value_gain):
    scaled, factor = normalize(tokens_in)
    normed = scaled.astype(jnp.bfloat16)
    spread = lax.all_to_all(normed, "tensor", split_axis=1, concat_axis=0, tiled=True)
    queries = heads_of(spread, query_gain)
    key_heads = heads_of(spread, key_gain)
    value_heads = heads_of(spread, value_gain)
    weights = softmax_causal(queries, key_heads).astype(jnp.bfloat16)
    mixed_out = jnp.einsum("hij,jhd->ihd", weights, value_heads, preferred_element_type=jnp.float32)
    mixed_out = mixed_out.astype(jnp.bfloat16).reshape(spread.shape)
    merged = lax.all_to_all(mixed_out, "tensor", split_axis=0, concat_axis=1, tiled=True)
    return (tokens_in.astype(jnp.float32) + merged.astype(jnp.float32)).astype(jnp.bfloat16)


def backward(stash_rows, grad_rows, query_gain, key_gain, value_gain):
    scaled, factor = normalize(stash_rows)
    normed = scaled.astype(jnp.bfloat16)
    spread, grad_heads = (
        lax.all_to_all(normed, "tensor", split_axis=1, concat_axis=0, tiled=True),
        lax.all_to_all(grad_rows, "tensor", split_axis=1, concat_axis=0, tiled=True),
    )
    queries = heads_of(spread, query_gain)
    key_heads = heads_of(spread, key_gain)
    value_heads = heads_of(spread, value_gain)
    cotangent = grad_heads.reshape(grad_heads.shape[0], -1, HDIM)
    weights = softmax_causal(queries, key_heads)
    weights_low = weights.astype(jnp.bfloat16)
    value_grad = jnp.einsum(
        "hij,ihd->jhd", weights_low, cotangent, preferred_element_type=jnp.float32
    )
    prob_grad = jnp.einsum(
        "ihd,jhd->hij", cotangent, value_heads, preferred_element_type=jnp.float32
    )
    score_grad = weights * (prob_grad - jnp.sum(prob_grad * weights, axis=-1, keepdims=True))
    score_low = score_grad.astype(jnp.bfloat16)
    query_grad = jnp.einsum(
        "hij,jhd->ihd", score_low, key_heads, preferred_element_type=jnp.float32
    )
    key_grad = jnp.einsum("hij,ihd->jhd", score_low, queries, preferred_element_type=jnp.float32)
    query_grad = query_grad * HDIM ** (-0.5)
    key_grad = key_grad * HDIM ** (-0.5)
    head_shape = spread.shape
    normed_grad = (
        query_grad.reshape(head_shape) * query_gain + key_grad.reshape(head_shape) * key_gain
    )
    normed_grad = (normed_grad + value_grad.reshape(head_shape) * value_gain).astype(jnp.bfloat16)
    returned = lax.all_to_all(
        normed_grad, "tensor", split_axis=0, concat_axis=1, tiled=True
    ).astype(jnp.float32)
    inner = jnp.mean(returned * scaled, axis=-1, keepdims=True)
    return (grad_rows.astype(jnp.float32) + factor * (returned - scaled * inner)).astype(
        jnp.bfloat16
    )


def bit_order(count):
    numbers = list(range(count))
    return numbers


def evict_chain(payload, numbers):
    for bit_number in numbers:
        payload = from_partner(payload, "section", bit_number)
    return payload


def reload_chain(payload, numbers):
    for bit_number in numbers:
        payload = from_partner(payload, "section", bit_number)
    return payload


def per_device(inflow, fresh, stash_held, grad_in, query_gain, key_gain, value_gain):
    numbers = bit_order(lax.axis_size("section").bit_length() - 1)
    gain_query = query_gain[0]
    gain_key = key_gain[0]
    gain_value = value_gain[0]
    first_out = forward(inflow[0], gain_query, gain_key, gain_value)
    moved = from_behind(first_out, "section", 1)
    second_in = jnp.where(lax.axis_index("section") == 0, fresh, moved)
    second_out = forward(second_in, gain_query, gain_key, gain_value)
    evicted = evict_chain(inflow[0], numbers)
    stash_rows = reload_chain(stash_held[0], numbers)
    grad_out = backward(stash_rows, grad_in[0], gain_query, gain_key, gain_value)
    return (first_out[None], second_out[None], evicted[None], grad_out[None])


def solution(mesh):
    placed = (
        P("section", "tensor", None),
        P("tensor", None),
        P("section", "tensor", None),
        P("section", "tensor", None),
        P("section", "tensor"),
        P("section", "tensor"),
        P("section", "tensor"),
    )
    return jax.shard_map(
        per_device,
        mesh=mesh,
        in_specs=placed,
        out_specs=(
            P("section", "tensor", None),
            P("section", "tensor", None),
            P("section", "tensor", None),
            P("section", "tensor", None),
        ),
        check_vma=False,
    )
```

profile of v0, /device:TPU:16, one launch (start us, length us, event | category | flops | bytes accessed | tf_op | source)
XLA Modules:
  0.0 708.8 jit_solution(6820127748169123507)
XLA Ops:
  0.6 3.5 copy.112
  8.1 4.6 copy.114
  12.7 5.2 all-to-all-start
  17.9 4.6 copy.132
  23.0 7.4 %all_to_all.77 = bf16[128,4,3072]{2,1,0:T(4,128)(2,1)} reshape(bf16[1,128,12288]{2,1,0:T(8,128)(2,1)} %param.10) | data formatting | bytes 6291456 | tf_op jit(solution)/shard_map/all_to_all | solution.py:67
  30.4 4.5 copy.136
  36.6 48.7 %all-to-all-done = bf16[128,4,3072]{2,0,1:T(8,128)(2,1)} async-done(((bf16[128,4,3072]{2,0,1:T(8,128)(2,1)}), bf16[128,4,3072]{2,0,1:T(8,128)(2,1)}, u32[]{:S(2)}, u32[]{:S(2)}) %all-to-all-start) | async-done | bytes 3145760 | tf_op jit(solution)/shard_map/all_to_all | solution.py:51
  85.3 8.2 %all-to-all-start.5 = ((bf16[128,4,3072]{2,0,1:T(8,128)(2,1)}), bf16[128,4,3072]{2,0,1:T(8,128)(2,1)}, u32[]{:S(2)}, u32[]{:S(2)}) async-start(bf16[128,4,3072]{2,0,1:T(8,128)(2,1)} %copy.136), calls=%async_computation.5 | async-start | bytes 6291456 | tf_op jit(solution)/shard_map/all_to_all | solution.py:67
  93.5 2.7 convert_element_type.256
  96.2 4.0 copy.161
  100.2 6.7 copy.115
  107.0 16.7 %fusion.37 = f32[24,512,512]{1,2,0:T(8,128)} fusion(f32[512,24,128]{0,2,1:T(8,128)} %copy.115, f32[24,128]{1,0:T(8,128)S(1)} %bitcast.104, f32[24,128]{1,0:T(8,128)S(1)} %bitcast.108), kind=kOutput, calls=%fused_computation.71 | convolution fusion | flops 1616904192 | bytes 31481856 | tf_op jit(solution)/shard_map/ihd,jhd->hij/dot_general | solution.py:37
  123.7 33.4 %fusion.62 = (f32[24,512]{1,0:T(8,128)S(1)}, f32[24,512,512]{1,2,0:T(8,128)}) fusion(f32[24,512,512]{1,2,0:T(8,128)} %fusion.37, pred[512,512]{0,1:T(8,128)(4,1)S(1)} %iota_compare_fusion), kind=kOutput, calls=%fused_computation.99 | output fusion | flops 37749248 | bytes 50642944 | tf_op jit(solution)/shard_map/sub | solution.py:44
  157.1 13.9 %convert_bitcast_fusion.3 = bf16[512,24,128]{0,2,1:T(8,128)(2,1)} fusion(f32[24,512,512]{1,2,0:T(8,128)} %get-tuple-element.21, f32[24,512]{1,0:T(8,128)S(1)} %get-tuple-element.20, f32[512,24,128]{0,2,1:T(8,128)} %copy.115, f32[24,128]{1,0:T(8,128)S(1)} %bitcast.112), kind=kOutput, calls=%fused_computation.75 | convolution fusion | flops 1627914240 | bytes 34664448 | tf_op jit(solution)/shard_map/hij,jhd->ihd/dot_general | solution.py:56
  171.0 5.7 all_to_all.34
  176.7 4.0 copy.121
  180.6 5.1 all-to-all-start.1
  188.8 4.7 copy.131
  193.4 4.6 copy.122
  198.0 4.5 copy.163
  202.5 51.8 %collective-permute-done.2 = bf16[128,12288]{0,1:T(8,128)(2,1)} collective-permute-done((bf16[128,12288]{0,1:T(8,128)(2,1)}, bf16[128,12288]{0,1:T(8,128)(2,1)}, u32[]{:S(2)}, u32[]{:S(2)}) %collective-permute-start.2) | collective-permute-done | bytes 3145760 | tf_op jit(solution)/shard_map/ppermute | solution.py:16
  256.5 3.1 fusion.32
  259.5 3.5 fusion.26
  263.0 3.0 collective-permute-start
  266.0 3.4 fusion.24
  269.4 5.1 all-to-all-start.4
  278.8 4.8 copy.146
  283.6 72.1 %collective-permute-done.3 = bf16[128,12288]{0,1:T(8,128)(2,1)} collective-permute-done((bf16[128,12288]{0,1:T(8,128)(2,1)}, bf16[128,12288]{0,1:T(8,128)(2,1)}, u32[]{:S(2)}, u32[]{:S(2)}) %collective-permute-start.3) | collective-permute-done | bytes 3145760 | tf_op jit(solution)/shard_map/ppermute | solution.py:16
  355.7 4.6 copy.148
  364.4 2.8 copy.123
  367.2 5.6 all-to-all-start.2
  375.1 14.3 %copy.133 = f32[4,128,3072]{1,0,2:T(4,128)} copy(f32[4,128,3072]{1,2,0:T(8,128)S(1)} %convert_bitcast_fusion.1) | data formatting | bytes 12582912 | tf_op jit(solution)/shard_map/convert_element_type | solution.py:32
  389.4 7.9 %reshape.208 = f32[512,24,128]{0,2,1:T(8,128)} reshape(f32[4,128,3072]{1,0,2:T(4,128)} %copy.133) | data formatting | bytes 12582912 | tf_op jit(solution)/shard_map/convert_element_type | solution.py:32
  397.3 4.5 multiply_convert_fusion.2
  401.8 15.3 %fusion.64 = (f32[24,512]{1,0:T(8,128)S(1)}, f32[24,512,512]{1,2,0:T(8,128)}) fusion(pred[512,512]{0,1:T(8,128)(4,1)S(1)} %iota_compare_fusion, bf16[512,24,128]{0,2,1:T(8,128)(2,1)} %get-tuple-element.19, bf16[512,24,128]{0,2,1:T(8,128)(2,1)S(1)} %get-tuple-element.18), kind=kOutput, calls=%fused_computation.101 | convolution fusion | flops 1635779072 | bytes 31768576 | tf_op jit(solution)/shard_map/sub | solution.py:44
  417.0 22.3 %fusion.3 = (f32[24,512]{1,0:T(8,128)S(1)}, f32[24,512,512]{2,1,0:T(8,128)}) fusion(f32[24,512,512]{1,2,0:T(8,128)} %get-tuple-element.25, f32[24,512]{1,0:T(8,128)S(1)} %get-tuple-element.24, bf16[512,24,128]{2,1,0:T(8,128)(2,1)} %bitcast.101, f32[512,24,128]{0,2,1:T(8,128)} %reshape.208, f32[24,128]{1,0:T(8,128)S(1)} %bitcast.113), kind=kOutput, calls=%fused_computation.5 | convolution fusion | flops 1632620544 | bytes 59879424 | tf_op jit(solution)/shard_map/ihd,jhd->hij/dot_general | solution.py:78
  439.4 16.3 %fusion.5 = bf16[24,512,512]{1,2,0:T(8,128)(2,1)S(1)} fusion(f32[24,512,512]{2,1,0:T(8,128)} %get-tuple-element.27, f32[24,512]{1,0:T(8,128)S(1)} %get-tuple-element.26, f32[24,512,512]{1,2,0:T(8,128)} %get-tuple-element.25, f32[24,512]{1,0:T(8,128)S(1)} %get-tuple-element.24), kind=kLoop, calls=%fused_computation.7 | loop fusion | flops 25165824 | bytes 63012864 | tf_op jit(solution)/shard_map/convert_element_type | solution.py:82
  455.7 4.5 copy-done
  460.2 4.5 multiply_bitcast_fusion.1
  464.7 12.3 %multiply_bitcast_fusion = f32[512,24,128]{0,2,1:T(8,128)} fusion(bf16[512,24,128]{0,2,1:T(8,128)(2,1)} %get-tuple-element.19, bf16[24,512,512]{1,2,0:T(8,128)(2,1)} %copy-done), kind=kOutput, calls=%fused_computation.59 | convolution fusion | flops 1612185600 | bytes 22020096 | tf_op jit(solution)/shard_map/hij,ihd->jhd/dot_general | solution.py:86
  477.0 7.6 %reshape.198 = f32[4,128,3072]{1,0,2:T(4,128)} reshape(f32[512,24,128]{0,2,1:T(8,128)} %multiply_bitcast_fusion.1) | data formatting | bytes 12582912 | tf_op jit(solution)/shard_map/reshape | solution.py:91
  484.5 7.6 %copy.140 = f32[4,128,3072]{2,1,0:T(8,128)} copy(f32[4,128,3072]{1,0,2:T(4,128)} %reshape.198) | data formatting | bytes 12582912 | tf_op jit(solution)/shard_map/reshape | solution.py:91
  492.1 7.5 %reshape.199 = f32[4,128,3072]{1,0,2:T(4,128)} reshape(f32[512,24,128]{0,2,1:T(8,128)} %multiply_bitcast_fusion) | data formatting | bytes 12582912 | tf_op jit(solution)/shard_map/reshape | solution.py:91
  499.7 7.7 %copy.142 = f32[4,128,3072]{2,1,0:T(8,128)} copy(f32[4,128,3072]{1,0,2:T(4,128)} %reshape.199) | data formatting | bytes 12582912 | tf_op jit(solution)/shard_map/reshape | solution.py:91
  507.4 10.0 %fusion.49 = f32[512,24,128]{2,0,1:T(8,128)S(1)} fusion(bf16[512,24,128]{2,1,0:T(8,128)(2,1)S(1)} %bitcast.102, f32[24,512,512]{1,2,0:T(8,128)} %get-tuple-element.25, f32[24,512]{1,0:T(8,128)S(1)} %get-tuple-element.24), kind=kOutput, calls=%fused_computation.86 | convolution fusion | flops 1623195648 | bytes 34652160 | tf_op jit(solution)/shard_map/hij,ihd->jhd/dot_general | solution.py:75
  517.4 6.3 copy.144
  523.7 7.2 %reshape.200 = f32[4,128,3072]{2,1,0:T(8,128)} reshape(f32[512,24,128]{2,1,0:T(8,128)} %copy.144) | data formatting | bytes 12582912 | tf_op jit(solution)/shard_map/reshape | solution.py:93
  530.9 10.5 %add_convert_fusion = bf16[4,128,3072]{2,1,0:T(8,128)(2,1)} fusion(f32[4,128,3072]{2,1,0:T(8,128)} %reshape.200, f32[4,128,3072]{2,1,0:T(8,128)} %copy.142, f32[4,128,3072]{2,1,0:T(8,128)} %copy.140, f32[3072]{0:T(1024)S(1)} %bitcast.114, f32[3072]{0:T(1024)S(1)} %bitcast.106, f32[3072]{0:T(1024)S(1)} %bitcast.110), kind=kLoop, calls=%fused_computation.58 | loop fusion | flops 9437184 | bytes 22056960 | tf_op jit(solution)/shard_map/convert_element_type | solution.py:93
  541.4 5.3 all-to-all-start.6
  549.4 4.0 copy.162
  553.4 6.7 copy.124
  560.1 16.5 %fusion.38 = f32[24,512,512]{1,2,0:T(8,128)} fusion(f32[512,24,128]{0,2,1:T(8,128)} %copy.124, f32[24,128]{1,0:T(8,128)S(1)} %bitcast.107, f32[24,128]{1,0:T(8,128)S(1)} %bitcast.111), kind=kOutput, calls=%fused_computation.72 | convolution fusion | flops 1616904192 | bytes 31481856 | tf_op jit(solution)/shard_map/ihd,jhd->hij/dot_general | solution.py:37
  576.6 33.1 %fusion.63 = (f32[24,512]{1,0:T(8,128)S(1)}, f32[24,512,512]{1,2,0:T(8,128)}) fusion(f32[24,512,512]{1,2,0:T(8,128)} %fusion.38, pred[512,512]{0,1:T(8,128)(4,1)S(1)} %copy-done.8), kind=kOutput, calls=%fused_computation.100 | output fusion | flops 37749248 | bytes 50642944 | tf_op jit(solution)/shard_map/sub | solution.py:44
  609.7 13.8 %convert_bitcast_fusion.2 = bf16[512,24,128]{0,2,1:T(8,128)(2,1)} fusion(f32[24,512,512]{1,2,0:T(8,128)} %get-tuple-element.23, f32[24,512]{1,0:T(8,128)S(1)} %get-tuple-element.22, f32[512,24,128]{0,2,1:T(8,128)} %copy.124, f32[24,128]{1,0:T(8,128)S(1)} %bitcast.115), kind=kOutput, calls=%fused_computation.74 | convolution fusion | flops 1627914240 | bytes 34664448 | tf_op jit(solution)/shard_map/hij,jhd->ihd/dot_general | solution.py:56
  623.5 4.0 all_to_all.73
  629.5 5.1 all-to-all-start.3
  634.6 5.3 convert_bitcast_fusion
  640.0 6.6 copy.145
  646.6 5.1 fusion.27
  653.0 4.2 fusion.31
  657.3 4.8 copy.149
  662.0 38.2 %all-to-all-done.3 = bf16[4,128,3072]{1,2,0:T(8,128)(2,1)} async-done(((bf16[4,128,3072]{1,2,0:T(8,128)(2,1)}), bf16[4,128,3072]{1,2,0:T(8,128)(2,1)}, u32[]{:S(2)}, u32[]{:S(2)}) %all-to-all-start.3) | async-done | bytes 3145760 | tf_op jit(solution)/shard_map/all_to_all | solution.py:58
  700.2 3.4 fusion.35
  703.7 4.6 copy.147
  (61 shorter events, 28.0 us)
Async XLA Ops:
  12.7 72.6 %all-to-all-start = ((bf16[128,4,3072]{2,0,1:T(8,128)(2,1)}), bf16[128,4,3072]{2,0,1:T(8,128)(2,1)}, u32[]{:S(2)}, u32[]{:S(2)}) async-start(bf16[128,4,3072]{2,0,1:T(8,128)(2,1)} %copy.114), calls=%async_computation | async-start | bytes 6291456 | tf_op jit(solution)/shard_map/all_to_all | solution.py:51
  22.5 12.5 %collective-permute-start.4 = (bf16[128,12288]{0,1:T(8,128)(2,1)}, bf16[128,12288]{0,1:T(8,128)(2,1)}, u32[]{:S(2)}, u32[]{:S(2)}) collective-permute-start(bf16[128,12288]{0,1:T(8,128)(2,1)} %bitcast.103), channel_id=1, source_target_pairs={{0,4},{4,0},{8,12},{12,8},{16,20},{20,16},{24,28},{28,24},{1,5},{5... | collective-permute-start | bytes 9437192 | tf_op jit(solution)/shard_map/ppermute | solution.py:16
  22.5 163.2 %collective-permute-start.1 = (bf16[128,12288]{0,1:T(8,128)(2,1)S(1)}, bf16[128,12288]{0,1:T(8,128)(2,1)}, u32[]{:S(2)}, u32[]{:S(2)}) collective-permute-start(bf16[128,12288]{0,1:T(8,128)(2,1)S(1)} %bitcast.91), channel_id=1, source_target_pairs={{0,4},{4,0},{8,12},{12,8},{16,20},{20,16},{24,28},{28,24},{1,5},{5... | collective-permute-start | bytes 9437192 | tf_op jit(solution)/shard_map/ppermute | solution.py:16
  35.0 366.8 %copy-start.7 = (pred[512,512]{0,1:T(8,128)(4,1)}, pred[512,512]{0,1:T(8,128)(4,1)S(1)}, u32[]{:S(2)}) copy-start(pred[512,512]{0,1:T(8,128)(4,1)S(1)} %iota_compare_fusion) | copy-start | bytes 786436
  35.0 152.2 %collective-permute-start.5 = (bf16[128,12288]{0,1:T(8,128)(2,1)}, bf16[128,12288]{0,1:T(8,128)(2,1)}, u32[]{:S(2)}, u32[]{:S(2)}) collective-permute-start(bf16[128,12288]{0,1:T(8,128)(2,1)} %collective-permute-done.4), channel_id=1, source_target_pairs={{0,8},{4,12},{8,0},{12,4},{16,24},{20,28},{24,16},{28,20},{1,9},{5... | collective-permute-start | bytes 9437192 | tf_op jit(solution)/shard_map/ppermute | solution.py:16
  85.3 95.3 %all-to-all-start.5 = ((bf16[128,4,3072]{2,0,1:T(8,128)(2,1)}), bf16[128,4,3072]{2,0,1:T(8,128)(2,1)}, u32[]{:S(2)}, u32[]{:S(2)}) async-start(bf16[128,4,3072]{2,0,1:T(8,128)(2,1)} %copy.136), calls=%async_computation.5 | async-start | bytes 6291456 | tf_op jit(solution)/shard_map/all_to_all | solution.py:67
  100.2 6.7 copy-start.9
  100.2 6.7 copy-start.11
  123.7 33.4 %copy-start.13 = (f32[1,3072]{1,0:T(1,128)S(1)}, f32[1,3072]{1,0:T(1,128)}, u32[]{:S(2)}) copy-start(f32[1,3072]{1,0:T(1,128)} %param.13) | copy-start | bytes 36868
  180.6 78.9 %all-to-all-start.1 = ((bf16[4,128,3072]{1,2,0:T(8,128)(2,1)}), bf16[4,128,3072]{1,2,0:T(8,128)(2,1)}, u32[]{:S(2)}, u32[]{:S(2)}) async-start(bf16[4,128,3072]{1,2,0:T(8,128)(2,1)} %copy.121), calls=%async_computation.1 | async-start | bytes 6291456 | tf_op jit(solution)/shard_map/all_to_all | solution.py:58
  185.7 68.6 %collective-permute-start.2 = (bf16[128,12288]{0,1:T(8,128)(2,1)}, bf16[128,12288]{0,1:T(8,128)(2,1)}, u32[]{:S(2)}, u32[]{:S(2)}) collective-permute-start(bf16[128,12288]{0,1:T(8,128)(2,1)} %collective-permute-done.1), channel_id=1, source_target_pairs={{0,8},{4,12},{8,0},{12,4},{16,24},{20,28},{24,16},{28,20},{1,9},{5... | collective-permute-start | bytes 9437192 | tf_op jit(solution)/shard_map/ppermute | solution.py:16
  187.2 69.2 %collective-permute-start.6 = (bf16[128,12288]{0,1:T(8,128)(2,1)}, bf16[128,12288]{0,1:T(8,128)(2,1)}, u32[]{:S(2)}, u32[]{:S(2)}) collective-permute-start(bf16[128,12288]{0,1:T(8,128)(2,1)} %collective-permute-done.5), channel_id=1, source_target_pairs={{0,16},{4,20},{8,24},{12,28},{16,0},{20,4},{24,8},{28,12},{1,17},{... | collective-permute-start | bytes 9437192 | tf_op jit(solution)/shard_map/ppermute | solution.py:16
  254.4 101.4 %collective-permute-start.3 = (bf16[128,12288]{0,1:T(8,128)(2,1)}, bf16[128,12288]{0,1:T(8,128)(2,1)}, u32[]{:S(2)}, u32[]{:S(2)}) collective-permute-start(bf16[128,12288]{0,1:T(8,128)(2,1)} %collective-permute-done.2), channel_id=1, source_target_pairs={{0,16},{4,20},{8,24},{12,28},{16,0},{20,4},{24,8},{28,12},{1,17},{... | collective-permute-start | bytes 9437192 | tf_op jit(solution)/shard_map/ppermute | solution.py:16
  259.5 9.9 %copy-start.14 = (f32[128]{0:T(128)}, f32[128]{0:T(128)S(1)}, u32[]{:S(2)}) copy-start(f32[128]{0:T(128)S(1)} %add_rsqrt_fusion) | copy-start | bytes 1540
  263.0 97.4 %collective-permute-start = (bf16[128,12288]{0,1:T(8,128)(2,1)}, bf16[128,12288]{0,1:T(8,128)(2,1)}, u32[]{:S(2)}, u32[]{:S(2)}) collective-permute-start(bf16[128,12288]{0,1:T(8,128)(2,1)} %fusion.26), channel_id=1, source_target_pairs={{0,4},{4,8},{8,12},{12,16},{16,20},{20,24},{24,28},{1,5},{5,9},{9,... | collective-permute-start | bytes 9437192 | tf_op jit(solution)/shard_map/ppermute | solution.py:22
  269.4 97.8 %all-to-all-start.4 = ((bf16[128,4,3072]{0,2,1:T(8,128)(2,1)}), bf16[128,4,3072]{0,2,1:T(8,128)(2,1)}, u32[]{:S(2)}, u32[]{:S(2)}) async-start(bf16[128,4,3072]{0,2,1:T(8,128)(2,1)} %bitcast.97), calls=%async_computation.4 | async-start | bytes 6291456 | tf_op jit(solution)/shard_map/all_to_all | solution.py:66
  278.8 81.6 %copy-start.4 = (bf16[128,12288]{0,1:T(8,128)(2,1)S(1)}, bf16[128,12288]{0,1:T(8,128)(2,1)}, u32[]{:S(2)}) copy-start(bf16[128,12288]{0,1:T(8,128)(2,1)} %copy.122) | copy-start | bytes 9437188
  362.1 1.7 copy-start.2
  367.2 174.2 %all-to-all-start.2 = ((bf16[128,4,3072]{2,0,1:T(8,128)(2,1)}), bf16[128,4,3072]{2,0,1:T(8,128)(2,1)}, u32[]{:S(2)}, u32[]{:S(2)}) async-start(bf16[128,4,3072]{2,0,1:T(8,128)(2,1)} %copy.123), calls=%async_computation.2 | async-start | bytes 6291456 | tf_op jit(solution)/shard_map/all_to_all | solution.py:51
  455.7 4.5 copy-start
  499.7 7.7 %copy-start.6 = (bf16[64,8,24,128]{3,2,1,0:T(8,128)(2,1)S(1)}, bf16[64,8,24,128]{3,2,1,0:T(8,128)(2,1)}, u32[]{:S(2)}) copy-start(bf16[64,8,24,128]{3,2,1,0:T(8,128)(2,1)} %copy.163) | copy-start | bytes 9437188
  523.7 7.2 %copy-start.10 = (f32[1,3072]{1,0:T(1,128)S(1)}, f32[1,3072]{1,0:T(1,128)}, u32[]{:S(2)}) copy-start(f32[1,3072]{1,0:T(1,128)} %param.12) | copy-start | bytes 36868
  523.7 7.2 %copy-start.12 = (f32[1,3072]{1,0:T(1,128)S(1)}, f32[1,3072]{1,0:T(1,128)}, u32[]{:S(2)}) copy-start(f32[1,3072]{1,0:T(1,128)} %param.11) | copy-start | bytes 36868
  541.4 88.2 %all-to-all-start.6 = ((bf16[4,128,3072]{2,1,0:T(8,128)(2,1)}), bf16[4,128,3072]{2,1,0:T(8,128)(2,1)}, u32[]{:S(2)}, u32[]{:S(2)}) async-start(bf16[4,128,3072]{2,1,0:T(8,128)(2,1)} %add_convert_fusion), calls=%async_computation.6 | async-start | bytes 6291456 | tf_op jit(solution)/shard_map/all_to_all | solution.py:94
  560.1 16.5 %copy-start.8 = (pred[512,512]{0,1:T(8,128)(4,1)S(1)}, pred[512,512]{0,1:T(8,128)(4,1)}, u32[]{:S(2)}) copy-start(pred[512,512]{0,1:T(8,128)(4,1)} %copy-done.7) | copy-start | bytes 786436
  629.5 70.7 %all-to-all-start.3 = ((bf16[4,128,3072]{1,2,0:T(8,128)(2,1)}), bf16[4,128,3072]{1,2,0:T(8,128)(2,1)}, u32[]{:S(2)}, u32[]{:S(2)}) async-start(bf16[4,128,3072]{1,2,0:T(8,128)(2,1)} %copy.130), calls=%async_computation.3 | async-start | bytes 6291456 | tf_op jit(solution)/shard_map/all_to_all | solution.py:58
  640.0 6.6 copy-start.15
  646.6 5.6 copy-start.1
  646.6 6.5 copy-start.5
  657.3 43.0 %copy-start.3 = (bf16[128,12288]{0,1:T(8,128)(2,1)S(1)}, bf16[128,12288]{0,1:T(8,128)(2,1)}, u32[]{:S(2)}) copy-start(bf16[128,12288]{0,1:T(8,128)(2,1)} %copy-done.2) | copy-start | bytes 9437188
where the time goes:
time: 720 us; the launch traced here: 709 us
  waiting for transfers between devices  212 us (29%)
  local copies, waits for them, and re-layouts  177 us (25%)
  other arithmetic  144 us (20%)
  matrix products  125 us (17%)
  starting transfers between devices  49.2 us (7%)
    ppermute x6, waiting for transfers between devices, from_partner(): return lax.ppermute(value, axis, pairs)  125 us
    sub x2, other arithmetic, softmax_causal(): weights = jnp.exp(scores - largest)  66.4 us
    unnamed x43, local copies, waits for them, and re-layouts  56.3 us
    all_to_all x2, waiting for transfers between devices, forward(): lax.all_to_all(normed, 'tensor', split_axis=1, concat_axis=0, tiled=True)  48.7 us
    all_to_all x2, waiting for transfers between devices, forward(): lax.all_to_all(mixed_out, 'tensor', split_axis=0, concat_axis=1, tiled=True)  38.2 us
    convert_element_type x4, local copies, waits for them, and re-layouts, heads_of(): scaled = (normed.astype(jnp.float32) * feature_gain).astype(jnp.bfloat16)  35.6 us
    dot_general x2, matrix products, softmax_causal(): jnp.einsum('ihd,jhd->hij', queries, key_heads, preferred_element_type=jnp...  33.3 us
    dot_general x2, matrix products, forward(): jnp.einsum('hij,jhd->ihd', weights, value_heads, preferred_element_type=j...  27.7 us
  transfers between devices with their start and end apart: 14, of which 5 were waited for; matrix products, arithmetic and copies ran while one was open for 57% of the time, Pallas kernels for 0%

commit v1 on v0

v1 whole, which is shorter than its diff:
```python
import functools
import math

import jax
import jax.numpy as jnp
from jax import lax
from jax.experimental import pallas as pl
from jax.experimental.pallas import tpu as pltpu
from jax.sharding import PartitionSpec as P

HDIM = 128
ROWS = 128
HEADS_PER_STEP = 2
AXES = ("section", "tensor")

epsilon = 1e-05
masked_score = -1e30
f32 = jnp.float32
bf16 = jnp.bfloat16


def nt(a, b):
    return lax.dot_general(a, b, (((1,), (1,)), ((), ())), preferred_element_type=f32)


def nn(a, b):
    return lax.dot_general(a, b, (((1,), (0,)), ((), ())), preferred_element_type=f32)


def tn(a, b):
    return lax.dot_general(a, b, (((0,), (0,)), ((), ())), preferred_element_type=f32)


def causal(scores, first_row):
    row = lax.broadcasted_iota(jnp.int32, scores.shape, 0) + first_row
    col = lax.broadcasted_iota(jnp.int32, scores.shape, 1)
    return jnp.where(row >= col, scores, masked_score)


def probabilities(scores):
    factor = HDIM ** (-0.5) * math.log2(math.e)
    largest = functools.reduce(
        jnp.maximum, [jnp.max(part, axis=-1, keepdims=True) for part in scores]
    )
    weights = [jnp.exp2((part - largest) * factor) for part in scores]
    total = sum(jnp.sum(part, axis=-1, keepdims=True) for part in weights)
    inverse = 1.0 / total
    return [part * inverse for part in weights]


def projections(x, factor, gains):
    normed = (x.astype(f32) * factor).astype(bf16).astype(f32)
    return [(normed * gain).astype(bf16) for gain in gains]


def forward_kernel(with_low, bias, own, own_r, low, low_r, qg, kg, vg, own_out, *low_out):
    offset = bias[...]
    for head in range(own.shape[1] // HDIM):
        cols = slice(head * HDIM, (head + 1) * HDIM)
        gains = [g[:, cols] for g in (qg, kg, vg)]
        query, key, value = projections(own[:, cols], own_r[...], gains)
        low_query, low_key, low_value = projections(low[:, cols], low_r[...], gains)
        for start in range(0, own.shape[0], ROWS):
            rows = slice(start, start + ROWS)
            seen = slice(0, start + ROWS)
            across = nt(query[rows], low_key) + offset
            within = causal(nt(query[rows], key[seen]), start)
            p_low, p_own = probabilities([across, within])
            mixed = nn(p_low.astype(bf16), low_value) + nn(p_own.astype(bf16), value[seen])
            mixed = mixed.astype(bf16).astype(f32)
            own_out[rows, cols] = (own[rows, cols].astype(f32) + mixed).astype(bf16)
            if with_low:
                within = causal(nt(low_query[rows], low_key[seen]), start)
                (p_own,) = probabilities([within])
                mixed = nn(p_own.astype(bf16), low_value[seen]).astype(bf16).astype(f32)
                low_out[0][rows, cols] = (low[rows, cols].astype(f32) + mixed).astype(bf16)


def backward_kernel(bias, own, own_r, low, low_r, grad, qg, kg, vg, own_out, low_out):
    offset = bias[...]
    scale = HDIM ** (-0.5)
    for head in range(own.shape[1] // HDIM):
        cols = slice(head * HDIM, (head + 1) * HDIM)
        gains = [g[:, cols] for g in (qg, kg, vg)]
        query, key, value = projections(own[:, cols], own_r[...], gains)
        _, low_key, low_value = projections(low[:, cols], low_r[...], gains)
        dlow = jnp.zeros(low_key.shape, f32)
        down = {}
        for start in range(0, own.shape[0], ROWS):
            rows = slice(start, start + ROWS)
            seen = slice(0, start + ROWS)
            g = grad[rows, cols]
            across = nt(query[rows], low_key) + offset
            within = causal(nt(query[rows], key[seen]), start)
            p_low, p_own = probabilities([across, within])
            d_low = nt(g, low_value)
            d_own = nt(g, value[seen])
            inner = jnp.sum(d_low * p_low, axis=-1, keepdims=True) + jnp.sum(
                d_own * p_own, axis=-1, keepdims=True
            )
            s_low = (p_low * (d_low - inner)).astype(bf16)
            s_own = (p_own * (d_own - inner)).astype(bf16)
            dquery = (nn(s_low, low_key) + nn(s_own, key[seen])) * scale
            low_part = tn(s_low, query[rows]) * (scale * gains[1])
            dlow = dlow + low_part + tn(p_low.astype(bf16), g) * gains[2]
            dkey = tn(s_own, query[rows]) * (scale * gains[1])
            dkey = dkey + tn(p_own.astype(bf16), g) * gains[2]
            for at in range(0, start + ROWS, ROWS):
                piece = dkey[at : at + ROWS]
                down[at] = down[at] + piece if at in down else piece
            down[start] = down[start] + dquery * gains[0]
        low_out[:, cols] = dlow.astype(bf16)
        for at, piece in down.items():
            own_out[at : at + ROWS, cols] = piece.astype(bf16)


def call_attention(kernel, outputs, bias, own, own_r, low, low_r, extra, gains):
    half, group = own.shape
    width = HDIM * HEADS_PER_STEP
    if group % width:
        width = HDIM
    wide = pl.BlockSpec((half, width), lambda i: (0, i))
    scalar = pl.BlockSpec((half, 1), lambda i: (0, 0))
    gain = pl.BlockSpec((1, width), lambda i: (0, i))
    return pl.pallas_call(
        kernel,
        grid=(group // width,),
        in_specs=[pl.BlockSpec((1, half), lambda i: (0, 0)), wide, scalar, wide, scalar]
        + [wide] * len(extra)
        + [gain] * 3,
        out_specs=[wide] * outputs,
        out_shape=[jax.ShapeDtypeStruct((half, group), bf16)] * outputs,
        compiler_params=pltpu.CompilerParams(vmem_limit_bytes=32 * 1024 * 1024),
        cost_estimate=pl.CostEstimate(
            flops=half * half * group * 12,
            bytes_accessed=half * group * 8,
            transcendentals=half * half * group // 50,
        ),
    )(bias, own, own_r, low, low_r, *extra, *gains)


def permute(value, route):
    sections, tensors = lax.axis_size("section"), lax.axis_size("tensor")
    pairs = []
    for s in range(sections):
        for z in range(tensors):
            target = route(s, z)
            if target is not None:
                pairs.append((s * tensors + z, target[0] * tensors + target[1]))
    return lax.ppermute(value, AXES, pairs)


def stay(s):
    return s


def first_only(s):
    return s if s == 0 else None


def routes(step, kind, to_section):
    tensors = lax.axis_size("tensor")
    half = tensors // 2

    def route(s, z):
        target = to_section(s)
        if target is None:
            return None
        base = z // half * half
        if kind == "up":
            if base:
                return None
            base = half
        elif kind == "down":
            if not base:
                return None
            base = 0
        return (target, base + (z % half + step) % half)

    return route


def spread(tokens, kind="within", to_section=stay):
    half = lax.axis_size("tensor") // 2
    place = lax.axis_index("tensor") % half
    rows, features = tokens.shape
    group = features // half
    result = jnp.zeros((half * rows, group), tokens.dtype)
    for step in range(half):
        piece = lax.dynamic_slice(tokens, (0, (place + step) % half * group), (rows, group))
        if kind != "within" or step:
            piece = permute(piece, routes(step, kind, to_section))
        result = lax.dynamic_update_slice(result, piece, ((place - step) % half * rows, 0))
    return result


def collect(heads, kind="within"):
    half = lax.axis_size("tensor") // 2
    place = lax.axis_index("tensor") % half
    length, group = heads.shape
    rows = length // half
    result = jnp.zeros((rows, half * group), heads.dtype)
    for step in range(half):
        piece = lax.dynamic_slice(heads, ((place + step) % half * rows, 0), (rows, group))
        if kind != "within" or step:
            piece = permute(piece, routes(step, kind, stay))
        result = lax.dynamic_update_slice(result, piece, (0, (place - step) % half * group))
    return result


def factor_of(tokens):
    values = tokens.astype(f32)
    return lax.rsqrt(jnp.mean(values * values, axis=-1) + epsilon)


def per_device(inflow, fresh, stash_held, grad_in, query_gain, key_gain, value_gain):
    sections, tensors = lax.axis_size("section"), lax.axis_size("tensor")
    section, place = lax.axis_index("section"), lax.axis_index("tensor")
    half = tensors // 2
    upper = place >= half
    inflow, held, grad = inflow[0], stash_held[0], grad_in[0]
    rows, features = inflow.shape
    length = half * rows

    def mirror(s):
        return sections - 1 - s

    inflow_own = spread(inflow)
    inflow_low = spread(inflow, "up")
    stash = permute(held, lambda s, z: (mirror(s), z))
    stash_low = spread(held, "up", mirror)
    grad_own = spread(grad)
    evicted = permute(inflow, lambda s, z: (mirror(s), z))
    fresh_own = spread(fresh, "within", first_only)
    fresh_low = spread(fresh, "up", first_only)

    factors = jnp.stack([factor_of(inflow), factor_of(held), factor_of(fresh)])
    factors = lax.all_gather(factors, "tensor", axis=1, tiled=True)
    stash_factors = permute(factors[1], lambda s, z: (mirror(s), z))

    def halves(values):
        low = values[:length, None]
        own = jnp.where(upper, values[length:, None], low)
        return own, low

    gains = jnp.concatenate([query_gain, key_gain, value_gain], axis=0)
    gains = lax.all_gather(gains, "tensor", axis=1, tiled=True)
    group = features // half
    gains = lax.dynamic_slice(gains, (0, place % half * group), (3, group))
    gains = [gains[i : i + 1] for i in range(3)]
    bias = jnp.where(upper, 0.0, masked_score).astype(f32) * jnp.ones((1, length), f32)

    own_r, low_r = halves(factors[0])
    first_own, first_low = call_attention(
        functools.partial(forward_kernel, True),
        2, bias, inflow_own, own_r, inflow_low, low_r, [], gains,
    )

    def onward(s, z):
        return (s + 1, z) if s + 1 < sections else None

    def onward_upper(s, z):
        return onward(s, z) if z >= half else None

    def squares(values):
        values = values.astype(f32)
        return jnp.sum(values * values, axis=-1)

    moved_own = permute(first_own, onward)
    moved_low = permute(first_low, onward_upper)
    sums = jnp.stack([squares(first_own), squares(first_low)])
    sums = lax.all_gather(sums, "tensor")
    sums = jnp.sum(lax.dynamic_slice_in_dim(sums, place // half * half, half, 0), axis=0)
    second_factors = permute(lax.rsqrt(sums / features + epsilon), onward)
    first_out = collect(first_own)

    stash_own = spread(stash)
    own_r, low_r = halves(stash_factors)
    dnormed_own, dnormed_low = call_attention(
        backward_kernel, 2, bias, stash_own, own_r, stash_low, low_r, [grad_own], gains
    )
    returned_low = collect(dnormed_low, "down")
    returned_own = collect(dnormed_own)

    is_first = section == 0
    own_r, low_r = halves(factors[2])
    second_own = jnp.where(is_first, fresh_own, moved_own)
    second_low = jnp.where(is_first, fresh_low, moved_low)
    own_r = jnp.where(is_first, own_r, second_factors[0][:, None])
    low_r = jnp.where(is_first, low_r, second_factors[1][:, None])
    (second_heads,) = call_attention(
        functools.partial(forward_kernel, False),
        1, bias, second_own, own_r, second_low, low_r, [], gains,
    )
    second_out = collect(second_heads)

    returned = returned_own.astype(f32) + returned_low.astype(f32)
    factor = factor_of(stash)[:, None]
    scaled = stash.astype(f32) * factor
    inner = jnp.mean(returned * scaled, axis=-1, keepdims=True)
    grad_out = (grad.astype(f32) + factor * (returned - scaled * inner)).astype(bf16)
    return (first_out[None], second_out[None], evicted[None], grad_out[None])


def solution(mesh):
    tokens = P("section", "tensor", None)
    gain = P("section", "tensor")
    return jax.shard_map(
        per_device,
        mesh=mesh,
        in_specs=(tokens, P("tensor", None), tokens, tokens, gain, gain, gain),
        out_specs=(tokens,) * 4,
        check_vma=False,
    )
```

time: 720 us -> 764 us (1.061); the launches traced: 709 us -> 761 us
  blocking collectives: 0 us -> 216 us
  Pallas kernels: 0 us -> 180 us
  matrix products: 125 us -> 0 us
  local copies, waits for them, and re-layouts: 177 us -> 55.3 us
  other arithmetic: 144 us -> 22.4 us
  starting transfers between devices: 49.2 us -> 143 us
  waiting for transfers between devices: 212 us -> 143 us
    all_gather x0 -> x3, blocking collectives: none -> 216 us  [the longest x1 137 us: per_device(): gains = lax.all_gather(gains, 'tensor', axis=1, tiled=True)]
    pallas_call x0 -> x3, Pallas kernels: none -> 180 us  [call_attention(): pl.pallas_call(kernel, grid=(group // width,), in_specs=[pl.BlockSpec((1,...]
    ppermute x7 -> x21, starting transfers between devices: 9.58 us -> 143 us  [permute(): return lax.ppermute(value, AXES, pairs)]
    dot_general x8 -> x0, matrix products: 110 us -> none  [the longest x2 33.3 us: softmax_causal(): jnp.einsum('ihd,jhd->hij', queries, key_heads, preferred_element_type=jnp...]
    all_to_all x7 -> x0, waiting for transfers between devices: 86.9 us -> none  [the longest x2 48.7 us: forward(): lax.all_to_all(normed, 'tensor', split_axis=1, concat_axis=0, tiled=True)]
    sub x2 -> x0, other arithmetic: 66.4 us -> none  [softmax_causal(): weights = jnp.exp(scores - largest)]
    convert_element_type x15 -> x0, other arithmetic: 66.1 us -> none  [the longest x1 16.3 us: backward(): score_low = score_grad.astype(jnp.bfloat16)]
    unnamed x43 -> x57, local copies, waits for them, and re-layouts: 56.3 us -> 9.08 us
  transfers between devices with their start and end apart: 14 -> 21, of which waited for: 5 -> 4; matrix products, arithmetic and copies ran while one was open for 57% -> 9% of each run, Pallas kernels for 0% -> 24%
where the time goes in v1:
time: 764 us; the launch traced here: 761 us
  blocking collectives  216 us (28%)
  Pallas kernels  180 us (24%)
  starting transfers between devices  143 us (19%)
  waiting for transfers between devices  143 us (19%)
  local copies, waits for them, and re-layouts  55.3 us (7%)
  other arithmetic  22.4 us (3%)
    pallas_call x3, Pallas kernels, call_attention(): pl.pallas_call(kernel, grid=(group // width,), in_specs=[pl.BlockSpec((1,...  180 us
    ppermute x21, starting transfers between devices, permute(): return lax.ppermute(value, AXES, pairs)  143 us
    ppermute x21, waiting for transfers between devices, permute(): return lax.ppermute(value, AXES, pairs)  143 us
    all_gather x1, blocking collectives, per_device(): gains = lax.all_gather(gains, 'tensor', axis=1, tiled=True)  137 us
    all_gather x1, blocking collectives, per_device(): factors = lax.all_gather(factors, 'tensor', axis=1, tiled=True)  68.7 us
    dynamic_update_slice x13, local copies, waits for them, and re-layouts, spread(): lax.dynamic_update_slice(result, piece, ((place - step) % half * rows, 0))  16.5 us
  transfers between devices with their start and end apart: 21, of which 4 were waited for; matrix products, arithmetic and copies ran while one was open for 9% of the time, Pallas kernels for 24%

profile of v1, /device:TPU:16, one launch (start us, length us, event | category | flops | bytes accessed | tf_op | source)
XLA Modules:
  0.0 761.2 jit_solution(6584659637531485293)
XLA Ops:
  0.7 2.8 dynamic-slice_bitcast_fusion.3
  3.5 1.3 collective-permute-start.2
  4.8 1.6 collective-permute-start
  6.4 2.6 multiply_reduce_fusion.4
  9.0 0.7 multiply_reduce_fusion.2
  9.7 2.6 multiply_reduce_fusion.3
  12.4 68.7 %all_gather.12 = f32[3,512]{1,0:T(4,128)S(1)} all-gather(f32[3,128]{1,0:T(4,128)S(1)} %pad_maximum_fusion.1), channel_id=1, replica_groups=mesh['section'=8,'tensor'=4] {'tensor'}, dimensions={1}, use_global_device_ids=true | all-gather | bytes 7680 | tf_op jit(solution)/shard_map/all_gather | solution.py:238
  81.4 2.0 constant_dynamic-update-slice_fusion.9
  83.4 1.3 collective-permute-start.8
  85.1 2.9 constant_dynamic-update-slice_fusion.14
  87.9 1.3 collective-permute-start.1
  89.2 3.9 dynamic-slice_bitcast_fusion.1
  93.2 2.8 dynamic-slice_bitcast_fusion
  96.0 137.0 %all_gather.13 = f32[3,12288]{1,0:T(4,128)} all-gather(f32[3,3072]{1,0:T(4,128)S(1)} %pad_maximum_fusion), channel_id=1, replica_groups=mesh['section'=8,'tensor'=4] {'tensor'}, dimensions={1}, use_global_device_ids=true | all-gather | bytes 184320 | tf_op jit(solution)/shard_map/all_gather | solution.py:247
  233.3 0.7 broadcast_select_fusion.2.own_r
  234.0 2.0 broadcast.128.clone.6
  236.0 1.2 bitcast_dynamic-update-slice_fusion
  237.3 1.8 fusion.12
  239.1 1.9 collective-permute-start.4
  241.4 1.4 collective-permute-start.15
  243.2 1.7 constant_dynamic-update-slice_fusion.12
  244.9 1.4 collective-permute-start.16
  246.4 1.6 constant_dynamic-update-slice_fusion.11.low
  248.0 2.1 collective-permute-start.17
  250.1 1.6 constant_dynamic-update-slice_fusion.13.own
  251.7 1.7 copy-done
  253.4 1.9 copy-done.1
  255.2 72.8 %shard_map.102 = (bf16[256,6144]{1,0:T(8,128)(2,1)S(1)}, bf16[256,6144]{1,0:T(8,128)(2,1)}) custom-call(f32[1,256]{1,0:T(1,128)S(1)} %mul.42.bias, bf16[256,6144]{1,0:T(8,128)(2,1)S(1)} %copy-done.1, f32[256,1]{1,0:T(8,128)S(1)} %copy-done.4, bf16[256,6144]{1,0:T(8,128)(2,1)S(1)} %constant_dynamic-update-slice_fusion.11.low, f32[256,1]{1,0:T(8,128)S(1)} %copy.19.low_r, ...), custom_call_target="tpu_custom_call" | custom-call | flops 4831838208 | bytes 12582912 | tf_op jit(solution)/shard_map/pallas_call | solution.py:125
  328.1 1.3 constant_dynamic-slice_fusion.9
  329.4 2.0 broadcast_in_dim.32.clone
  331.3 1.2 bitcast_dynamic-update-slice_fusion.4
  332.6 3.2 multiply_reduce_fusion
  335.8 10.6 %all-gather.1 = f32[4,2,256]{2,1,0:T(2,128)S(1)} all-gather(f32[1,2,256]{2,1,0:T(2,128)S(1)} %maximum_bitcast_fusion), channel_id=2, replica_groups=mesh['section'=8,'tensor'=4] {'tensor'}, dimensions={0}, use_global_device_ids=true | all-gather | bytes 10240 | tf_op jit(solution)/shard_map/all_gather | solution.py:272
  346.4 2.6 collective-permute-start.12
  349.6 1.3 collective-permute-start.7
  351.4 1.6 constant_dynamic-update-slice_fusion.1.grad
  353.0 23.6 %collective-permute-done.7 = bf16[128,6144]{1,0:T(8,128)(2,1)S(1)} collective-permute-done((bf16[128,6144]{1,0:T(8,128)(2,1)S(1)}, bf16[128,6144]{1,0:T(8,128)(2,1)S(1)}, u32[]{:S(2)}, u32[]{:S(2)}) %collective-permute-start.7) | collective-permute-done | bytes 1572896 | tf_op jit(solution)/shard_map/ppermute | solution.py:150
  376.6 3.0 collective-permute-start.9
  380.2 1.6 collective-permute-start.6
  381.8 1.6 constant_dynamic-update-slice_fusion.6
  383.4 13.7 %collective-permute-start.3 = (bf16[128,6144]{1,0:T(8,128)(2,1)}, bf16[128,6144]{1,0:T(8,128)(2,1)}, u32[]{:S(2)}, u32[]{:S(2)}) collective-permute-start(bf16[128,6144]{1,0:T(8,128)(2,1)} %constant_dynamic-slice_fusion.9), channel_id=1, source_target_pairs={{0,1},{1,0},{2,3},{3,2},{4,5},{5,4},{6,7},{7,6},{8,9},{9,8},{10,11... | collective-permute-start | bytes 4718600 | tf_op jit(solution)/shard_map/ppermute | solution.py:150
  397.1 1.6 constant_dynamic-update-slice_fusion.8
  398.7 101.6 %collective-permute-start.5 = (bf16[256,6144]{1,0:T(8,128)(2,1)S(1)}, bf16[256,6144]{1,0:T(8,128)(2,1)}, u32[]{:S(2)}, u32[]{:S(2)}) collective-permute-start(bf16[256,6144]{1,0:T(8,128)(2,1)S(1)} %get-tuple-element.8), channel_id=1, source_target_pairs={{0,4},{1,5},{2,6},{3,7},{4,8},{5,9},{6,10},{7,11},{8,12},{9,13},{1... | collective-permute-start | bytes 9437192 | tf_op jit(solution)/shard_map/ppermute | solution.py:150
  500.3 0.6 fusion.11
  500.9 0.8 copy.21.own_r
  501.7 0.8 copy.22.low_r
  502.9 2.2 constant_dynamic-slice_fusion.3
  505.1 1.1 collective-permute-start.13
  506.2 2.7 bitcast_dynamic-update-slice_fusion.3
  508.9 2.7 fusion.7
  511.7 30.7 %collective-permute-done.13 = bf16[128,6144]{1,0:T(8,128)(2,1)S(1)} collective-permute-done((bf16[128,6144]{1,0:T(8,128)(2,1)S(1)}, bf16[128,6144]{1,0:T(8,128)(2,1)S(1)}, u32[]{:S(2)}, u32[]{:S(2)}) %collective-permute-start.13) | collective-permute-done | bytes 1572896 | tf_op jit(solution)/shard_map/ppermute | solution.py:150
  542.5 66.4 %shard_map.104 = (bf16[256,6144]{1,0:T(8,128)(2,1)S(1)}, bf16[256,6144]{1,0:T(8,128)(2,1)S(1)}) custom-call(f32[1,256]{1,0:T(1,128)S(1)} %mul.42.bias, bf16[256,6144]{1,0:T(8,128)(2,1)S(1)} %constant_dynamic-update-slice_fusion.4.own, f32[256,1]{1,0:T(8,128)S(1)} %copy.23.own_r, bf16[256,6144]{1,0:T(8,128)(2,1)S(1)} %copy-done.3, f32[256,1]{1,0:T(8,128)S(1)} %copy.24.low_r, ...), custom_call_target="tpu_custom_call" | custom-call | flops 4831838208 | bytes 12582912 | tf_op jit(solution)/shard_map/pallas_call | solution.py:125
  609.5 1.1 collective-permute-start.18
  611.0 1.5 collective-permute-start.19
  612.5 1.7 collective-permute-start.20
  614.6 0.4 broadcast_select_fusion.1.own
  615.1 0.4 copy-done.5
  615.5 41.1 %shard_map.103 = bf16[256,6144]{1,0:T(8,128)(2,1)S(1)} custom-call(f32[1,256]{1,0:T(1,128)S(1)} %mul.42.bias, bf16[256,6144]{1,0:T(8,128)(2,1)S(1)} %broadcast_select_fusion.1.own, f32[256,1]{1,0:T(8,128)S(1)} %copy.21.own_r, bf16[256,6144]{1,0:T(8,128)(2,1)S(1)} %broadcast_select_fusion.low, f32[256,1]{1,0:T(8,128)S(1)} %copy-done.5, ...), custom_call_target="tpu_custom_call" | custom-call | flops 4831838208 | bytes 12582912 | tf_op jit(solution)/shard_map/pallas_call | solution.py:125
  656.8 1.1 collective-permute-start.10
  658.6 56.0 %collective-permute-done.19 = bf16[128,6144]{1,0:T(8,128)(2,1)S(1)} collective-permute-done((bf16[128,6144]{1,0:T(8,128)(2,1)S(1)}, bf16[128,6144]{1,0:T(8,128)(2,1)S(1)}, u32[]{:S(2)}, u32[]{:S(2)}) %collective-permute-start.19) | collective-permute-done | bytes 1572896 | tf_op jit(solution)/shard_map/ppermute | solution.py:150
  715.1 32.2 %collective-permute-done.20 = bf16[128,6144]{1,0:T(8,128)(2,1)S(1)} collective-permute-done((bf16[128,6144]{1,0:T(8,128)(2,1)S(1)}, bf16[128,6144]{1,0:T(8,128)(2,1)S(1)}, u32[]{:S(2)}, u32[]{:S(2)}) %collective-permute-start.20) | collective-permute-done | bytes 1572896 | tf_op jit(solution)/shard_map/ppermute | solution.py:150
  747.6 3.6 fusion.2
  751.2 4.8 fusion.8
  756.2 5.0 copy.48
  (112 shorter events, 7.0 us)
Async XLA Ops:
  0.7 8.4 %copy-start.12 = (bf16[128,12288]{1,0:T(8,128)(2,1)S(1)}, bf16[128,12288]{1,0:T(8,128)(2,1)}, u32[]{:S(2)}) copy-start(bf16[128,12288]{1,0:T(8,128)(2,1)} %param.8) | copy-start | bytes 9437188
  3.5 241.4 %collective-permute-start.2 = (bf16[128,6144]{1,0:T(8,128)(2,1)}, bf16[128,6144]{1,0:T(8,128)(2,1)}, u32[]{:S(2)}, u32[]{:S(2)}) collective-permute-start(bf16[128,6144]{1,0:T(8,128)(2,1)} %dynamic-slice_bitcast_fusion.3), channel_id=1, source_target_pairs={{0,3},{1,2},{4,7},{5,6},{8,11},{9,10},{12,15},{13,14},{16,19},{17,... | collective-permute-start | bytes 4718600 | tf_op jit(solution)/shard_map/ppermute | solution.py:150
  4.8 243.2 %collective-permute-start = (bf16[128,6144]{1,0:T(8,128)(2,1)}, bf16[128,6144]{1,0:T(8,128)(2,1)}, u32[]{:S(2)}, u32[]{:S(2)}) collective-permute-start(bf16[128,6144]{1,0:T(8,128)(2,1)} %dynamic-slice_bitcast_fusion.3), channel_id=1, source_target_pairs={{0,1},{1,0},{2,3},{3,2},{4,5},{5,4},{6,7},{7,6},{8,9},{9,8},{10,11... | collective-permute-start | bytes 4718600 | tf_op jit(solution)/shard_map/ppermute | solution.py:150
  81.1 158.0 %collective-permute-start.14 = (f32[512]{0:T(512)S(1)}, f32[512]{0:T(512)S(1)}, u32[]{:S(2)}, u32[]{:S(2)}) collective-permute-start(f32[512]{0:T(512)S(1)} %bitcast.56), channel_id=1, source_target_pairs={{0,28},{1,29},{2,30},{3,31},{4,24},{5,25},{6,26},{7,27},{8,20},{9,... | collective-permute-start | bytes 6152 | tf_op jit(solution)/shard_map/ppermute | solution.py:150
  83.4 4.5 copy-start.13
  83.4 296.7 %collective-permute-start.8 = (bf16[128,6144]{1,0:T(8,128)(2,1)}, bf16[128,6144]{1,0:T(8,128)(2,1)}, u32[]{:S(2)}, u32[]{:S(2)}) collective-permute-start(bf16[128,6144]{1,0:T(8,128)(2,1)} %get-tuple-element.24), channel_id=1, source_target_pairs={{0,3},{1,2}} | collective-permute-start | bytes 4718600 | tf_op jit(solution)/shard_map/ppermute | solution.py:150
  87.9 153.4 %collective-permute-start.1 = (bf16[128,6144]{1,0:T(8,128)(2,1)}, bf16[128,6144]{1,0:T(8,128)(2,1)}, u32[]{:S(2)}, u32[]{:S(2)}) collective-permute-start(bf16[128,6144]{1,0:T(8,128)(2,1)} %get-tuple-element.15), channel_id=1, source_target_pairs={{0,2},{1,3},{4,6},{5,7},{8,10},{9,11},{12,14},{13,15},{16,18},{17,... | collective-permute-start | bytes 4718600 | tf_op jit(solution)/shard_map/ppermute | solution.py:150
  93.2 2.8 copy-start.25
  93.2 2.8 copy-start.26
  93.2 2.8 copy-start.27
  233.3 2.7 copy-start.19
  239.1 144.3 %collective-permute-start.4 = (bf16[128,6144]{1,0:T(8,128)(2,1)}, bf16[128,6144]{1,0:T(8,128)(2,1)}, u32[]{:S(2)}, u32[]{:S(2)}) collective-permute-start(bf16[128,6144]{1,0:T(8,128)(2,1)} %get-tuple-element.24), channel_id=1, source_target_pairs={{0,1},{1,0},{2,3},{3,2}} | collective-permute-start | bytes 4718600 | tf_op jit(solution)/shard_map/ppermute | solution.py:150
  241.3 3.5 copy-start.24
  241.4 105.0 %collective-permute-start.15 = (bf16[128,6144]{1,0:T(8,128)(2,1)}, bf16[128,6144]{1,0:T(8,128)(2,1)S(1)}, u32[]{:S(2)}, u32[]{:S(2)}) collective-permute-start(bf16[128,6144]{1,0:T(8,128)(2,1)} %get-tuple-element.21), channel_id=1, source_target_pairs={{0,30},{1,31},{4,26},{5,27},{8,22},{9,23},{12,18},{13,19},{16,14},... | collective-permute-start | bytes 4718600 | tf_op jit(solution)/shard_map/ppermute | solution.py:150
  243.1 4.8 copy-start.23
  244.9 8.4 %copy-start.4 = (f32[256,1]{1,0:T(8,128)S(1)}, f32[256,1]{1,0:T(8,128)}, u32[]{:S(2)}) copy-start(f32[256,1]{1,0:T(8,128)} %broadcast_select_fusion.2.own_r) | copy-start | bytes 3076
  244.9 8.4 %copy-start.6 = (f32[1,6144]{1,0:T(1,128)S(1)}, f32[1,6144]{1,0:T(1,128)}, u32[]{:S(2)}) copy-start(f32[1,6144]{1,0:T(1,128)} %get-tuple-element.25.vg) | copy-start | bytes 73732
  244.9 8.4 %copy-start.8 = (f32[1,6144]{1,0:T(1,128)S(1)}, f32[1,6144]{1,0:T(1,128)}, u32[]{:S(2)}) copy-start(f32[1,6144]{1,0:T(1,128)} %get-tuple-element.26.kg) | copy-start | bytes 73732
  244.9 8.4 %copy-start.10 = (f32[1,6144]{1,0:T(1,128)S(1)}, f32[1,6144]{1,0:T(1,128)}, u32[]{:S(2)}) copy-start(f32[1,6144]{1,0:T(1,128)} %get-tuple-element.27.qg) | copy-start | bytes 73732
  244.9 104.7 %collective-permute-start.16 = (bf16[128,6144]{1,0:T(8,128)(2,1)S(1)}, bf16[128,6144]{1,0:T(8,128)(2,1)S(1)}, u32[]{:S(2)}, u32[]{:S(2)}) collective-permute-start(bf16[128,6144]{1,0:T(8,128)(2,1)S(1)} %copy-done.24), channel_id=1, source_target_pairs={{0,31},{1,30},{4,27},{5,26},{8,23},{9,22},{12,19},{13,18},{16,15},... | collective-permute-start | bytes 4718600 | tf_op jit(solution)/shard_map/ppermute | solution.py:150
  248.0 103.1 %collective-permute-start.17 = (bf16[128,6144]{1,0:T(8,128)(2,1)S(1)}, bf16[128,6144]{1,0:T(8,128)(2,1)S(1)}, u32[]{:S(2)}, u32[]{:S(2)}) collective-permute-start(bf16[128,6144]{1,0:T(8,128)(2,1)S(1)} %copy-done.23), channel_id=1, source_target_pairs={{0,1},{1,0},{2,3},{3,2},{4,5},{5,4},{6,7},{7,6},{8,9},{9,8},{10,11... | collective-permute-start | bytes 4718600 | tf_op jit(solution)/shard_map/ppermute | solution.py:150
  251.7 1.7 copy-start
  253.4 1.9 copy-start.1
  346.4 3.2 copy-start.22
  346.4 156.1 %collective-permute-start.12 = (bf16[128,12288]{1,0:T(8,128)(2,1)}, bf16[128,12288]{1,0:T(8,128)(2,1)}, u32[]{:S(2)}, u32[]{:S(2)}) collective-permute-start(bf16[128,12288]{1,0:T(8,128)(2,1)} %bitcast.4), channel_id=1, source_target_pairs={{0,28},{1,29},{2,30},{3,31},{4,24},{5,25},{6,26},{7,27},{8,20},{9,... | collective-permute-start | bytes 9437192 | tf_op jit(solution)/shard_map/ppermute | solution.py:150
  349.6 27.0 %collective-permute-start.7 = (bf16[128,6144]{1,0:T(8,128)(2,1)S(1)}, bf16[128,6144]{1,0:T(8,128)(2,1)S(1)}, u32[]{:S(2)}, u32[]{:S(2)}) collective-permute-start(bf16[128,6144]{1,0:T(8,128)(2,1)S(1)} %copy-done.22), channel_id=1, source_target_pairs={{0,2},{1,3}} | collective-permute-start | bytes 4718600 | tf_op jit(solution)/shard_map/ppermute | solution.py:150
  351.1 28.8 %copy-start.2 = (bf16[256,6144]{1,0:T(8,128)(2,1)}, bf16[256,6144]{1,0:T(8,128)(2,1)S(1)}, u32[]{:S(2)}) copy-start(bf16[256,6144]{1,0:T(8,128)(2,1)S(1)} %constant_dynamic-update-slice_fusion.2.low) | copy-start | bytes 9437188
  351.1 155.1 %collective-permute-start.11 = (bf16[128,12288]{1,0:T(8,128)(2,1)}, bf16[128,12288]{1,0:T(8,128)(2,1)}, u32[]{:S(2)}, u32[]{:S(2)}) collective-permute-start(bf16[128,12288]{1,0:T(8,128)(2,1)} %bitcast.2), channel_id=1, source_target_pairs={{0,28},{1,29},{2,30},{3,31},{4,24},{5,25},{6,26},{7,27},{8,20},{9,... | collective-permute-start | bytes 9437192 | tf_op jit(solution)/shard_map/ppermute | solution.py:150
  376.6 237.6 %collective-permute-start.9 = (bf16[256,6144]{1,0:T(8,128)(2,1)}, bf16[256,6144]{1,0:T(8,128)(2,1)}, u32[]{:S(2)}, u32[]{:S(2)}) collective-permute-start(bf16[256,6144]{1,0:T(8,128)(2,1)} %get-tuple-element.9), channel_id=1, source_target_pairs={{2,6},{3,7},{6,10},{7,11},{10,14},{11,15},{14,18},{15,19},{18,22},... | collective-permute-start | bytes 9437192 | tf_op jit(solution)/shard_map/ppermute | solution.py:150
  379.9 17.2 %copy-start.14 = (bf16[256,6144]{1,0:T(8,128)(2,1)S(1)}, bf16[256,6144]{1,0:T(8,128)(2,1)}, u32[]{:S(2)}) copy-start(bf16[256,6144]{1,0:T(8,128)(2,1)} %copy-done.13) | copy-start | bytes 9437188
  380.2 18.6 %collective-permute-start.6 = (f32[2,256]{1,0:T(2,128)S(1)}, f32[2,256]{1,0:T(2,128)S(1)}, u32[]{:S(2)}, u32[]{:S(2)}) collective-permute-start(f32[2,256]{1,0:T(2,128)S(1)} %add_rsqrt_fusion), channel_id=1, source_target_pairs={{0,4},{1,5},{2,6},{3,7},{4,8},{5,9},{6,10},{7,11},{8,12},{9,13},{1... | collective-permute-start | bytes 6152 | tf_op jit(solution)/shard_map/ppermute | solution.py:150
  383.4 117.5 %copy-start.17 = (bf16[256,6144]{1,0:T(8,128)(2,1)}, bf16[256,6144]{1,0:T(8,128)(2,1)S(1)}, u32[]{:S(2)}) copy-start(bf16[256,6144]{1,0:T(8,128)(2,1)S(1)} %constant_dynamic-update-slice_fusion.6) | copy-start | bytes 9437188
  383.4 122.8 %collective-permute-start.3 = (bf16[128,6144]{1,0:T(8,128)(2,1)}, bf16[128,6144]{1,0:T(8,128)(2,1)}, u32[]{:S(2)}, u32[]{:S(2)}) collective-permute-start(bf16[128,6144]{1,0:T(8,128)(2,1)} %constant_dynamic-slice_fusion.9), channel_id=1, source_target_pairs={{0,1},{1,0},{2,3},{3,2},{4,5},{5,4},{6,7},{7,6},{8,9},{9,8},{10,11... | collective-permute-start | bytes 4718600 | tf_op jit(solution)/shard_map/ppermute | solution.py:150
  398.7 102.2 %copy-start.15 = (bf16[256,6144]{1,0:T(8,128)(2,1)}, bf16[256,6144]{1,0:T(8,128)(2,1)S(1)}, u32[]{:S(2)}) copy-start(bf16[256,6144]{1,0:T(8,128)(2,1)S(1)} %constant_dynamic-update-slice_fusion.8) | copy-start | bytes 9437188
  398.7 215.9 %collective-permute-start.5 = (bf16[256,6144]{1,0:T(8,128)(2,1)S(1)}, bf16[256,6144]{1,0:T(8,128)(2,1)}, u32[]{:S(2)}, u32[]{:S(2)}) collective-permute-start(bf16[256,6144]{1,0:T(8,128)(2,1)S(1)} %get-tuple-element.8), channel_id=1, source_target_pairs={{0,4},{1,5},{2,6},{3,7},{4,8},{5,9},{6,10},{7,11},{8,12},{9,13},{1... | collective-permute-start | bytes 9437192 | tf_op jit(solution)/shard_map/ppermute | solution.py:150
  505.1 37.2 %collective-permute-start.13 = (bf16[128,6144]{1,0:T(8,128)(2,1)S(1)}, bf16[128,6144]{1,0:T(8,128)(2,1)S(1)}, u32[]{:S(2)}, u32[]{:S(2)}) collective-permute-start(bf16[128,6144]{1,0:T(8,128)(2,1)S(1)} %get-tuple-element.22), channel_id=1, source_target_pairs={{0,1},{1,0},{2,3},{3,2},{4,5},{5,4},{6,7},{7,6},{8,9},{9,8},{10,11... | collective-permute-start | bytes 4718600 | tf_op jit(solution)/shard_map/ppermute | solution.py:150
  508.9 33.6 %copy-start.3 = (bf16[256,6144]{1,0:T(8,128)(2,1)S(1)}, bf16[256,6144]{1,0:T(8,128)(2,1)}, u32[]{:S(2)}) copy-start(bf16[256,6144]{1,0:T(8,128)(2,1)} %copy-done.2) | copy-start | bytes 9437188
  508.9 33.6 %copy-start.7 = (f32[1,6144]{1,0:T(1,128)S(1)}, f32[1,6144]{1,0:T(1,128)}, u32[]{:S(2)}) copy-start(f32[1,6144]{1,0:T(1,128)} %get-tuple-element.25.vg) | copy-start | bytes 73732
  508.9 33.6 %copy-start.9 = (f32[1,6144]{1,0:T(1,128)S(1)}, f32[1,6144]{1,0:T(1,128)}, u32[]{:S(2)}) copy-start(f32[1,6144]{1,0:T(1,128)} %get-tuple-element.26.kg) | copy-start | bytes 73732
  508.9 33.6 %copy-start.11 = (f32[1,6144]{1,0:T(1,128)S(1)}, f32[1,6144]{1,0:T(1,128)}, u32[]{:S(2)}) copy-start(f32[1,6144]{1,0:T(1,128)} %get-tuple-element.27.qg) | copy-start | bytes 73732
  609.5 48.8 %collective-permute-start.18 = (bf16[128,6144]{1,0:T(8,128)(2,1)S(1)}, bf16[128,6144]{1,0:T(8,128)(2,1)S(1)}, u32[]{:S(2)}, u32[]{:S(2)}) collective-permute-start(bf16[128,6144]{1,0:T(8,128)(2,1)S(1)} %get-tuple-element.16), channel_id=1, source_target_pairs={{0,1},{1,0},{2,3},{3,2},{4,5},{5,4},{6,7},{7,6},{8,9},{9,8},{10,11... | collective-permute-start | bytes 4718600 | tf_op jit(solution)/shard_map/ppermute | solution.py:150
  610.6 3.5 copy-start.18
  611.0 103.6 %collective-permute-start.19 = (bf16[128,6144]{1,0:T(8,128)(2,1)S(1)}, bf16[128,6144]{1,0:T(8,128)(2,1)S(1)}, u32[]{:S(2)}, u32[]{:S(2)}) collective-permute-start(bf16[128,6144]{1,0:T(8,128)(2,1)S(1)} %get-tuple-element.19), channel_id=1, source_target_pairs={{2,0},{3,1},{6,4},{7,5},{10,8},{11,9},{14,12},{15,13},{18,16},{19,... | collective-permute-start | bytes 4718600 | tf_op jit(solution)/shard_map/ppermute | solution.py:150
  612.5 2.1 copy-start.16
  612.5 134.8 %collective-permute-start.20 = (bf16[128,6144]{1,0:T(8,128)(2,1)S(1)}, bf16[128,6144]{1,0:T(8,128)(2,1)S(1)}, u32[]{:S(2)}, u32[]{:S(2)}) collective-permute-start(bf16[128,6144]{1,0:T(8,128)(2,1)S(1)} %get-tuple-element.18), channel_id=1, source_target_pairs={{2,1},{3,0},{6,5},{7,4},{10,9},{11,8},{14,13},{15,12},{18,17},{19,... | collective-permute-start | bytes 4718600 | tf_op jit(solution)/shard_map/ppermute | solution.py:150
  614.6 0.9 copy-start.5
  656.8 99.2 %collective-permute-start.10 = (bf16[128,6144]{1,0:T(8,128)(2,1)S(1)}, bf16[128,6144]{1,0:T(8,128)(2,1)S(1)}, u32[]{:S(2)}, u32[]{:S(2)}) collective-permute-start(bf16[128,6144]{1,0:T(8,128)(2,1)S(1)} %constant_dynamic-slice_fusion.4), channel_id=1, source_target_pairs={{0,1},{1,0},{2,3},{3,2},{4,5},{5,4},{6,7},{7,6},{8,9},{9,8},{10,11... | collective-permute-start | bytes 4718600 | tf_op jit(solution)/shard_map/ppermute | solution.py:150
  747.6 3.6 copy-start.20
  756.2 5.0 copy-start.21

commit v2 on v0

v2 whole, which is shorter than its diff:
```python
import functools
import math

import jax
import jax.numpy as jnp
from jax import lax
from jax.experimental import pallas as pl
from jax.experimental.pallas import tpu as pltpu
from jax.sharding import PartitionSpec as P

HDIM = 128
ROWS = 128
LANES = 128
CHUNKS = 2
MESH = pl.DeviceIdType.MESH

epsilon = 1e-05
masked_score = -1e30
f32 = jnp.float32
bf16 = jnp.bfloat16


def nt(a, b):
    return lax.dot_general(a, b, (((1,), (1,)), ((), ())), preferred_element_type=f32)


def nn(a, b):
    return lax.dot_general(a, b, (((1,), (0,)), ((), ())), preferred_element_type=f32)


def projections(x, factor, gains):
    normed = (x.astype(f32) * factor).astype(bf16).astype(f32)
    return [(normed * gain).astype(bf16) for gain in gains]


def exponentials(keys, queries):
    factor = HDIM ** (-0.5) * math.log2(math.e)
    scores = nt(keys, queries)
    count = queries.shape[0]
    before = scores.shape[0] - count
    row = lax.broadcasted_iota(jnp.int32, (count, count), 1)
    col = lax.broadcasted_iota(jnp.int32, (count, count), 0)
    last = jnp.where(row >= col, scores[before:], masked_score)
    if before:
        scores = jnp.concatenate([scores[:before], last], axis=0)
    else:
        scores = last
    largest = jnp.max(scores, axis=0, keepdims=True)
    weights = jnp.exp2((scores - largest) * factor)
    return weights, 1.0 / jnp.sum(weights, axis=0, keepdims=True)


def attend(x, out, sums, cols, query, key, value, base):
    turned = value.T
    for start in range(0, query.shape[0], ROWS):
        rows = slice(start, start + ROWS)
        seen = base + start + ROWS
        weights, inverse = exponentials(key[:seen], query[rows])
        mixed = (nn(turned[:, :seen], weights.astype(bf16)) * inverse).T
        mixed = mixed.astype(bf16).astype(f32)
        result = (x[rows, cols].astype(f32) + mixed).astype(bf16)
        out[rows, cols] = result
        if sums is not None:
            result = result.astype(f32)
            sums[rows, :] += result * result


def derive(grad, cols, query, key, value, base, gains):
    scale = HDIM ** (-0.5)
    turned = key.T
    total = {}
    for start in range(0, query.shape[0], ROWS):
        rows = slice(start, start + ROWS)
        seen = base + start + ROWS
        g = grad[rows, cols]
        weights, inverse = exponentials(key[:seen], query[rows])
        weights = weights * inverse
        dprob = nt(value[:seen], g)
        inner = jnp.sum(dprob * weights, axis=0, keepdims=True)
        dscore = (weights * (dprob - inner)).astype(bf16)
        dquery = nn(turned[:, :seen], dscore).T * (scale * gains[0])
        part = nn(dscore, query[rows]) * (scale * gains[1])
        part = part + nn(weights.astype(bf16), g) * gains[2]
        for at in range(0, seen, ROWS):
            piece = part[at : at + ROWS]
            if at == seen - ROWS:
                piece = piece + dquery
            total[at] = total[at] + piece if at in total else piece
    return total


def each_head(begin, width, body):
    count = width // HDIM
    together = 2 if count % 2 == 0 else 1

    def step(index, carry):
        for offset in range(together):
            at = begin + (index * together + offset) * HDIM
            body(pl.ds(pl.multiple_of(at, HDIM), HDIM))
        return carry

    lax.fori_loop(0, count // together, step, 0)


def kernel(
    sections, tensors,
    inflow, fresh, held, grad, inflow_sums, fresh_sums, held_sums, gains_in,
    first_out, second_out, evicted, stash, returned_own, returned_low,
    x_own, x_low, st_own, st_low, g_own, m_own, m_low, f_own, f_low, dn_own, dn_low, s_own,
    xs_own, xs_low, ss_own, ss_low, ms_own, ms_low, fs_own, fs_low, gains,
    send_sems, recv_sems, local_sems,
):
    half = tensors // 2
    rows, features = inflow.shape
    length = half * rows
    group = features // half
    part = group // CHUNKS
    section, place = lax.axis_index("section"), lax.axis_index("tensor")
    mirror = sections - 1 - section
    inner = lax.rem(place, half)
    base = place - inner
    upper = place >= half
    lower = place < half
    is_first = section == 0
    has_next = section + 1 < sections
    has_before = section > 0
    always = None
    counters = {"remote": 0, "local": 0}
    pending = []

    def guarded(condition, action):
        if condition is always:
            action()
        else:
            pl.when(condition)(action)

    def both(a, b):
        return a if b is always else b if a is always else jnp.logical_and(a, b)

    class Copy:
        def __init__(self, source, there, landing, target, sends=always, gets=always):
            index = counters["remote"]
            counters["remote"] += 1
            self.sends, self.gets = sends, gets
            self.out = pltpu.make_async_remote_copy(
                src_ref=source, dst_ref=there, send_sem=send_sems.at[index],
                recv_sem=recv_sems.at[index], device_id=target, device_id_type=MESH,
            )
            self.into = pltpu.make_async_remote_copy(
                src_ref=landing, dst_ref=landing, send_sem=send_sems.at[index],
                recv_sem=recv_sems.at[index], device_id=target, device_id_type=MESH,
            )
            pending.append(self)

        def start(self):
            guarded(self.sends, self.out.start)

        def receive(self):
            guarded(self.gets, self.into.wait_recv)

        def sent(self):
            if self in pending:
                pending.remove(self)
                guarded(self.sends, self.out.wait_send)

    class Local:
        def __init__(self, source, target, condition=always):
            index = counters["local"]
            counters["local"] += 1
            self.condition = condition
            self.copy = pltpu.make_async_copy(source, target, local_sems.at[index])

        def start(self):
            guarded(self.condition, self.copy.start)

        def receive(self):
            guarded(self.condition, self.copy.wait)

        def sent(self):
            pass

    def turn(step):
        return lax.rem(inner + step, half), lax.rem(inner + half - step, half)

    def columns(which, chunk):
        return pl.ds(pl.multiple_of(which * group + chunk * part, LANES), part)

    def block(which):
        return pl.ds(pl.multiple_of(which * rows, 16), rows)

    def to_heads(tokens, heads, chunk, kind, to_section, condition=always):
        copies = []
        own_cols = pl.ds(chunk * part, part)
        for step in range(half):
            ahead, behind = turn(step)
            source = tokens.at[:, columns(ahead, chunk)]
            there = heads.at[block(inner), own_cols]
            landing = heads.at[block(behind), own_cols]
            if kind == "up":
                copies.append(Copy(
                    source, there, landing, (to_section, half + ahead),
                    both(lower, condition), both(upper, condition),
                ))
            elif step == 0:
                copies.append(Local(source, there, condition))
            else:
                copies.append(Copy(source, there, landing, (to_section, base + ahead), condition, condition))
        return copies

    def to_tokens(heads, tokens, chunk, kind):
        copies = []
        own_cols = pl.ds(chunk * part, part)
        for step in range(half):
            ahead, behind = turn(step)
            source = heads.at[block(ahead), own_cols]
            there = tokens.at[:, columns(inner, chunk)]
            landing = tokens.at[:, columns(behind, chunk)]
            if kind == "down":
                copies.append(Copy(source, there, landing, (section, ahead), upper, lower))
            elif step == 0:
                copies.append(Local(source, there))
            else:
                copies.append(Copy(source, there, landing, (section, base + ahead)))
        return copies

    def sums_to(source, target, kind, to_section, condition=always):
        copies = []
        for step in range(half):
            ahead, behind = turn(step)
            there, landing = target(inner), target(behind)
            if kind == "up":
                copies.append(Copy(
                    source, there, landing, (to_section, half + ahead),
                    both(lower, condition), both(upper, condition),
                ))
            elif step == 0 and kind == "within":
                copies.append(Local(source, there, condition))
            else:
                copies.append(Copy(source, there, landing, (to_section, base + ahead), condition, condition))
        return copies

    def run(copies):
        for copy in copies:
            copy.start()
        return copies

    def arrive(*lists):
        for copies in lists:
            for copy in copies:
                copy.receive()

    def left(copies):
        for copy in copies:
            copy.sent()

    barrier = pltpu.get_barrier_semaphore()

    def greet(to_section, to_place):
        pl.semaphore_signal(barrier, inc=1, device_id=(to_section, to_place), device_id_type=MESH)

    for step in range(1, tensors):
        greet(section, lax.rem(place + step, tensors))
    for step in range(tensors):
        greet(mirror, lax.rem(place + step, tensors))

    @pl.when(has_next)
    def _():
        for step in range(half):
            greet(section + 1, base + turn(step)[0])

    @pl.when(has_before)
    def _():
        for step in range(half):
            greet(section - 1, base + turn(step)[0])

    neighbours = has_next.astype(jnp.int32) + has_before.astype(jnp.int32)
    pl.semaphore_wait(barrier, 2 * tensors - 1 + half * neighbours)

    share = features // tensors
    pair = place // 2
    gain_copies = []
    for parity in range(2):
        there = gains.at[:, pl.ds(parity * share, share)]
        mine = lax.rem(place, 2) == parity
        for to in (0, half):
            target = to + pair
            self_copy = both(mine, target == place)
            from_me = 2 * inner + parity == place
            in_half = base == to
            gain_copies.append(Copy(
                gains_in, there, there, (section, target),
                both(mine, target != place), both(in_half, jnp.logical_not(from_me)),
            ))
            gain_copies.append(Local(gains_in, there, self_copy))
    run(gain_copies)

    def rows_of(ref):
        return lambda which: ref.at[block(which)]

    def slots_of(ref):
        return lambda which: ref.at[:, block(which)]

    inflow_factors = run(
        sums_to(inflow_sums, rows_of(xs_low), "up", section) + sums_to(inflow_sums, rows_of(xs_own), "within", section)
    )
    up_inflow = [to_heads(inflow, x_low, chunk, "up", section) for chunk in range(CHUNKS)]
    own_inflow = [to_heads(inflow, x_own, chunk, "within", section) for chunk in range(CHUNKS)]
    run(up_inflow[0] + own_inflow[0])
    mirror_stash = run([Copy(held, stash, stash, (mirror, place))])
    run(up_inflow[1] + own_inflow[1])
    stash_factors = run(
        sums_to(held_sums, rows_of(ss_low), "up", mirror) + sums_to(held_sums, rows_of(ss_own), "away", mirror)
    )
    own_grad = [to_heads(grad, g_own, chunk, "within", section) for chunk in range(CHUNKS)]
    up_stash = [to_heads(held, st_low, chunk, "up", mirror) for chunk in range(CHUNKS)]
    own_stash = [to_heads(stash, st_own, chunk, "within", section) for chunk in range(CHUNKS)]
    up_fresh = [to_heads(fresh, m_low, chunk, "up", section, is_first) for chunk in range(CHUNKS)]
    own_fresh = [to_heads(fresh, m_own, chunk, "within", section, is_first) for chunk in range(CHUNKS)]
    fresh_factors = sums_to(fresh_sums, slots_of(ms_low), "up", section, is_first) + sums_to(
        fresh_sums, slots_of(ms_own), "within", section, is_first
    )
    mirror_inflow = [Copy(inflow, evicted, evicted, (mirror, place))]

    fs_own[...] = jnp.zeros_like(fs_own)
    fs_low[...] = jnp.zeros_like(fs_low)

    def factor(total):
        return lax.rsqrt(jnp.sum(total, axis=-1, keepdims=True) / features + epsilon)

    def gains_of(cols):
        return [gains[i : i + 1, cols] for i in range(3)]

    def forward(chunk, own, low, own_total, low_total, own_out, low_out, own_sums, low_sums):
        @pl.when(upper)
        def _():
            own_factor, low_factor = factor(own_total()), factor(low_total())

            def head(cols):
                g = gains_of(cols)
                query, key, value = projections(own[:, cols], own_factor, g)
                low_query, low_key, low_value = projections(low[:, cols], low_factor, g)
                keys = jnp.concatenate([low_key, key], axis=0)
                values = jnp.concatenate([low_value, value], axis=0)
                attend(own, own_out, own_sums, cols, query, keys, values, length)
                if low_out is not None:
                    attend(low, low_out, low_sums, cols, low_query, low_key, low_value, 0)

            each_head(chunk * part, part, head)

        @pl.when(lower)
        def _():
            own_factor = factor(own_total())

            def head(cols):
                query, key, value = projections(own[:, cols], own_factor, gains_of(cols))
                attend(own, own_out, own_sums, cols, query, key, value, 0)

            each_head(chunk * part, part, head)

    def backward(chunk):
        @pl.when(upper)
        def _():
            own_factor, low_factor = factor(ss_own[...]), factor(ss_low[...])

            def head(cols):
                g = gains_of(cols)
                query, key, value = projections(st_own[:, cols], own_factor, g)
                low_key, low_value = projections(st_low[:, cols], low_factor, g[1:])
                keys = jnp.concatenate([low_key, key], axis=0)
                values = jnp.concatenate([low_value, value], axis=0)
                for at, piece in derive(g_own, cols, query, keys, values, length, g).items():
                    if at < length:
                        dn_low[at : at + ROWS, cols] = piece.astype(bf16)
                    else:
                        dn_own[at - length : at - length + ROWS, cols] = piece.astype(bf16)

            each_head(chunk * part, part, head)

        @pl.when(lower)
        def _():
            own_factor = factor(ss_own[...])

            def head(cols):
                g = gains_of(cols)
                query, key, value = projections(st_own[:, cols], own_factor, g)
                for at, piece in derive(g_own, cols, query, key, value, 0, g).items():
                    dn_own[at : at + ROWS, cols] = piece.astype(bf16)

            each_head(chunk * part, part, head)

    next_upper = both(has_next, upper)
    before_upper = both(has_before, upper)
    relays, firsts = [], []
    for chunk in range(CHUNKS):
        if chunk == 0:
            arrive(gain_copies, inflow_factors)
        arrive(up_inflow[chunk], own_inflow[chunk])
        forward(
            chunk, x_own, x_low, lambda: xs_own[...], lambda: xs_low[...],
            f_own, f_low, fs_own, fs_low,
        )
        cols = pl.ds(chunk * part, part)
        relays += run([
            Copy(f_own.at[:, cols], m_own.at[:, cols], m_own.at[:, cols], (section + 1, place), has_next, has_before),
            Copy(f_low.at[:, cols], m_low.at[:, cols], m_low.at[:, cols], (section + 1, place), next_upper, before_upper),
        ])
        left(up_inflow[chunk])
        run(up_stash[chunk])
        if chunk == 0:
            arrive(mirror_stash)
        run(own_grad[chunk] + own_stash[chunk])
        firsts += run(to_tokens(f_own, first_out, chunk, "within"))

    for step in range(half):
        ahead, behind = turn(step)
        relays += run([
            Copy(fs_own, ms_own.at[inner], ms_own.at[behind], (section + 1, base + ahead), has_next, has_before),
            Copy(fs_low, ms_low.at[inner], ms_low.at[behind], (section + 1, base + ahead), next_upper, before_upper),
        ])
    run(mirror_inflow)

    backs = []
    for chunk in range(CHUNKS):
        if chunk == 0:
            arrive(stash_factors)
        arrive(up_stash[chunk], own_grad[chunk], own_stash[chunk])
        left(up_stash[chunk])
        run(up_fresh[chunk] + own_fresh[chunk])
        if chunk == 0:
            run(fresh_factors)
        backward(chunk)
        backs += run(to_tokens(dn_low, returned_low, chunk, "down") + to_tokens(dn_own, returned_own, chunk, "within"))

    arrive(relays, fresh_factors, *up_fresh, *own_fresh)
    seconds = []
    for chunk in range(CHUNKS):
        forward(
            chunk, m_own, m_low, lambda: jnp.sum(ms_own[...], axis=0), lambda: jnp.sum(ms_low[...], axis=0),
            s_own, None, None, None,
        )
        seconds += run(to_tokens(s_own, second_out, chunk, "within"))
    arrive(firsts, mirror_inflow, backs, seconds)
    for copy in list(pending):
        copy.sent()


def counts(half):
    remote = CHUNKS * (9 * half + 2) + 9 * half + 16
    return remote, CHUNKS * 8 + 16


def row_sums(tokens):
    values = tokens.astype(f32)
    return jnp.pad(jnp.sum(values * values, axis=-1, keepdims=True), ((0, 0), (0, LANES - 1)))


def per_device(inflow, fresh, stash_held, grad_in, query_gain, key_gain, value_gain):
    sections, tensors = lax.axis_size("section"), lax.axis_size("tensor")
    half = tensors // 2
    inflow, held, grad = inflow[0], stash_held[0], grad_in[0]
    rows, features = inflow.shape
    length, group = half * rows, features // half
    gains_in = jnp.pad(
        jnp.concatenate([query_gain, key_gain, value_gain], axis=0), ((0, 5), (0, 0))
    )
    fresh_sums = jnp.pad(row_sums(fresh)[None], ((0, half - 1), (0, 0), (0, 0)))
    tokens = jax.ShapeDtypeStruct((rows, features), bf16)
    any_space = pl.BlockSpec(memory_space=pl.ANY)
    wide = pltpu.VMEM((length, group), bf16)
    narrow = pltpu.VMEM((length, LANES), f32)
    slots = pltpu.VMEM((half, length, LANES), f32)
    remote, local = counts(half)
    first_out, second_out, evicted, stash, returned_own, returned_low = pl.pallas_call(
        functools.partial(kernel, sections, tensors),
        in_specs=[any_space] * 8,
        out_specs=[any_space] * 6,
        out_shape=[tokens] * 6,
        scratch_shapes=[wide] * 12
        + [narrow] * 4
        + [slots] * 2
        + [narrow] * 2
        + [pltpu.VMEM((8, group), f32)]
        + [
            pltpu.SemaphoreType.DMA((remote,)),
            pltpu.SemaphoreType.DMA((remote,)),
            pltpu.SemaphoreType.DMA((local,)),
        ],
        compiler_params=pltpu.CompilerParams(
            collective_id=0, has_side_effects=True, vmem_limit_bytes=54 * 1024 * 1024
        ),
        cost_estimate=pl.CostEstimate(
            flops=length * length * group * 40,
            bytes_accessed=length * group * 40,
            transcendentals=length * length * group // 16,
        ),
    )(inflow, fresh, held, grad, row_sums(inflow), fresh_sums, row_sums(held), gains_in)

    received = lax.axis_index("tensor") < half
    returned = returned_own.astype(f32) + jnp.where(received, returned_low.astype(f32), 0.0)
    values = stash.astype(f32)
    factor = lax.rsqrt(jnp.mean(values * values, axis=-1, keepdims=True) + epsilon)
    scaled = values * factor
    inner = jnp.mean(returned * scaled, axis=-1, keepdims=True)
    grad_out = (grad.astype(f32) + factor * (returned - scaled * inner)).astype(bf16)
    return (first_out[None], second_out[None], evicted[None], grad_out[None])


def solution(mesh):
    tokens = P("section", "tensor", None)
    gain = P("section", "tensor")
    return jax.shard_map(
        per_device,
        mesh=mesh,
        in_specs=(tokens, P("tensor", None), tokens, tokens, gain, gain, gain),
        out_specs=(tokens,) * 4,
        check_vma=False,
    )
```

time: 720 us -> 485 us (0.67); the launches traced: 709 us -> 485 us
  Pallas kernels: 0 us -> 457 us
  waiting for transfers between devices: 212 us -> 0 us
  local copies, waits for them, and re-layouts: 177 us -> 11.3 us
  other arithmetic: 144 us -> 15.9 us
  matrix products: 125 us -> 0 us
  starting transfers between devices: 49.2 us -> 0 us
    pallas_call x0 -> x1, Pallas kernels: none -> 457 us  [per_device(): pl.pallas_call(functools.partial(kernel, sections, tensors), in_specs=[an...]
    ppermute x7 -> x0, waiting for transfers between devices: 125 us -> none  [the longest x6 125 us: from_partner(): return lax.ppermute(value, axis, pairs)]
    dot_general x8 -> x0, matrix products: 110 us -> none  [the longest x2 33.3 us: softmax_causal(): jnp.einsum('ihd,jhd->hij', queries, key_heads, preferred_element_type=jnp...]
    all_to_all x7 -> x0, waiting for transfers between devices: 86.9 us -> none  [the longest x2 48.7 us: forward(): lax.all_to_all(normed, 'tensor', split_axis=1, concat_axis=0, tiled=True)]
    sub x2 -> x0, other arithmetic: 66.4 us -> none  [softmax_causal(): weights = jnp.exp(scores - largest)]
    convert_element_type x15 -> x0, other arithmetic: 66.1 us -> none  [the longest x1 16.3 us: backward(): score_low = score_grad.astype(jnp.bfloat16)]
    unnamed x43 -> x27, local copies, waits for them, and re-layouts: 56.3 us -> 8.96 us
    convert_element_type x6 -> x0, local copies, waits for them, and re-layouts: 46.8 us -> none  [the longest x4 35.6 us: heads_of(): scaled = (normed.astype(jnp.float32) * feature_gain).astype(jnp.bfloat16)]
  transfers between devices with their start and end apart: 14 -> 0, of which waited for: 5 -> 0; matrix products, arithmetic and copies ran while one was open for 57% -> 0% of each run, Pallas kernels for 0% -> 0%
where the time goes in v2:
time: 485 us
  Pallas kernels  457 us (94%)
  other arithmetic  15.9 us (3%)
  local copies, waits for them, and re-layouts  11.3 us (2%)
    pallas_call x1, Pallas kernels, per_device(): pl.pallas_call(functools.partial(kernel, sections, tensors), in_specs=[an...  457 us

profile of v2, /device:TPU:16, one launch (start us, length us, event | category | flops | bytes accessed | tf_op | source)
XLA Modules:
  0.0 484.8 jit_solution(9180897376563446499)
XLA Ops:
  0.6 0.0 copy-start.6
  0.6 0.0 copy-start.7
  0.7 2.7 multiply_reduce_fusion.2
  3.4 0.1 copy-done.6
  3.5 0.0 copy-start.9
  3.5 0.0 copy-start.10
  3.5 0.0 copy-start.11
  3.5 0.7 multiply_reduce_fusion.1
  4.2 0.3 copy-done.7
  4.4 0.7 multiply_reduce_fusion
  5.1 0.1 copy.13
  5.2 0.6 pad.21.held_sums
  5.9 0.1 copy.12
  6.0 0.1 copy.11
  6.1 0.6 pad.18.inflow_sums
  6.8 0.7 pad.20.fresh_sums
  7.4 0.0 copy-done.9
  7.4 0.0 copy-done.10
  7.4 0.0 copy-done.11
  7.4 0.7 select_maximum_fusion.gains_in
  8.1 456.9 %shard_map.102 = (bf16[128,12288]{1,0:T(8,128)(2,1)}, bf16[128,12288]{1,0:T(8,128)(2,1)}, bf16[128,12288]{1,0:T(8,128)(2,1)}, bf16[128,12288]{1,0:T(8,128)(2,1)}...) custom-call(bf16[128,12288]{1,0:T(8,128)(2,1)} %bitcast.19, bf16[128,12288]{1,0:T(8,128)(2,1)} %fresh.1, ...), custom_call_target="tpu_custom_call" | custom-call | flops 16106127360 | bytes 62914560 | tf_op jit(solution)/shard_map/pallas_call | solution.py:473
  465.0 0.0 copy-start
  465.0 2.7 fusion.7
  467.8 0.1 copy-done
  467.9 0.0 copy-start.1
  467.9 0.0 copy-start.2
  467.9 0.0 copy-start.8
  467.9 4.8 fusion.2
  472.7 0.0 copy-done.1
  472.7 0.0 copy-done.2
  472.7 0.8 copy-done.8
  473.5 0.0 copy-start.5
  473.5 3.6 fusion.8
  477.1 0.0 copy-done.5
  477.1 0.0 copy-start.4
  477.1 1.7 copy.17
  478.7 1.4 copy-done.4
  480.1 0.0 copy-start.3
  480.1 1.7 copy.18
  481.7 1.4 copy-done.3
  483.1 1.7 copy.19
  (3 shorter events, 0.0 us)
Async XLA Ops:
  0.6 2.8 copy-start.6
  0.6 3.8 copy-start.7
  3.5 4.0 copy-start.9
  3.5 4.0 copy-start.10
  3.5 4.0 copy-start.11
  465.0 2.8 copy-start
  467.9 4.8 copy-start.1
  467.9 4.8 copy-start.2
  467.9 5.6 %copy-start.8 = (bf16[1,128,12288]{2,1,0:T(8,128)(2,1)S(1)}, bf16[1,128,12288]{2,1,0:T(8,128)(2,1)}, u32[]{:S(2)}) copy-start(bf16[1,128,12288]{2,1,0:T(8,128)(2,1)} %param.10) | copy-start | bytes 9437188
  473.5 3.6 copy-start.5
  477.1 3.0 copy-start.4
  480.1 3.0 copy-start.3

commit v3 on v2

--- a/solution.py
+++ b/solution.py
@@ -11,7 +11,7 @@
 HDIM = 128
 ROWS = 128
 LANES = 128
-CHUNKS = 2
+CHUNKS = 3
 MESH = pl.DeviceIdType.MESH
 
 epsilon = 1e-05
@@ -104,10 +104,11 @@
 
 def kernel(
     sections, tensors,
-    inflow, fresh, held, grad, inflow_sums, fresh_sums, held_sums, gains_in,
+    inflow, fresh, held, grad, gains_in,
     first_out, second_out, evicted, stash, returned_own, returned_low,
     x_own, x_low, st_own, st_low, g_own, m_own, m_low, f_own, f_low, dn_own, dn_low, s_own,
     xs_own, xs_low, ss_own, ss_low, ms_own, ms_low, fs_own, fs_low, gains,
+    inflow_here, held_here, fresh_here, inflow_sums, held_sums, fresh_sums,
     send_sems, recv_sems, local_sems,
 ):
     half = tensors // 2
@@ -300,19 +301,19 @@
     def slots_of(ref):
         return lambda which: ref.at[:, block(which)]
 
-    inflow_factors = run(
-        sums_to(inflow_sums, rows_of(xs_low), "up", section) + sums_to(inflow_sums, rows_of(xs_own), "within", section)
+    loads = run([Local(inflow, inflow_here), Local(held, held_here), Local(fresh, fresh_here)])
+    inflow_factors = sums_to(inflow_sums, rows_of(xs_low), "up", section) + sums_to(
+        inflow_sums, rows_of(xs_own), "within", section
     )
     up_inflow = [to_heads(inflow, x_low, chunk, "up", section) for chunk in range(CHUNKS)]
     own_inflow = [to_heads(inflow, x_own, chunk, "within", section) for chunk in range(CHUNKS)]
     run(up_inflow[0] + own_inflow[0])
     mirror_stash = run([Copy(held, stash, stash, (mirror, place))])
-    run(up_inflow[1] + own_inflow[1])
-    stash_factors = run(
-        sums_to(held_sums, rows_of(ss_low), "up", mirror) + sums_to(held_sums, rows_of(ss_own), "away", mirror)
+    stash_factors = sums_to(held_sums, rows_of(ss_low), "up", mirror) + sums_to(
+        held_sums, rows_of(ss_own), "away", mirror
     )
     own_grad = [to_heads(grad, g_own, chunk, "within", section) for chunk in range(CHUNKS)]
-    up_stash = [to_heads(held, st_low, chunk, "up", mirror) for chunk in range(CHUNKS)]
+    up_stash = [to_heads(stash, st_low, chunk, "up", section) for chunk in range(CHUNKS)]
     own_stash = [to_heads(stash, st_own, chunk, "within", section) for chunk in range(CHUNKS)]
     up_fresh = [to_heads(fresh, m_low, chunk, "up", section, is_first) for chunk in range(CHUNKS)]
     own_fresh = [to_heads(fresh, m_own, chunk, "within", section, is_first) for chunk in range(CHUNKS)]
@@ -321,6 +322,26 @@
     )
     mirror_inflow = [Copy(inflow, evicted, evicted, (mirror, place))]
 
+    def add_squares(tokens, sums):
+        sums[...] = jnp.zeros_like(sums)
+
+        def tile(cols):
+            values = tokens[:, cols].astype(f32)
+            sums[...] += values * values
+
+        each_head(0, features, tile)
+
+    arrive(loads)
+    add_squares(inflow_here, inflow_sums)
+    run(inflow_factors)
+    for chunk in range(1, CHUNKS):
+        run(up_inflow[chunk] + own_inflow[chunk])
+    add_squares(held_here, held_sums)
+    run(stash_factors)
+    for chunk in range(CHUNKS):
+        run(own_grad[chunk])
+    fresh_sums[...] = jnp.zeros_like(fresh_sums)
+    add_squares(fresh_here, fresh_sums.at[0])
     fs_own[...] = jnp.zeros_like(fs_own)
     fs_low[...] = jnp.zeros_like(fs_low)
 
@@ -395,6 +416,12 @@
         if chunk == 0:
             arrive(gain_copies, inflow_factors)
         arrive(up_inflow[chunk], own_inflow[chunk])
+        if chunk == 0:
+            arrive(mirror_stash)
+        left(up_inflow[chunk])
+        run(up_stash[chunk] + own_stash[chunk])
+        if chunk == 0:
+            run(mirror_inflow)
         forward(
             chunk, x_own, x_low, lambda: xs_own[...], lambda: xs_low[...],
             f_own, f_low, fs_own, fs_low,
@@ -404,11 +431,6 @@
             Copy(f_own.at[:, cols], m_own.at[:, cols], m_own.at[:, cols], (section + 1, place), has_next, has_before),
             Copy(f_low.at[:, cols], m_low.at[:, cols], m_low.at[:, cols], (section + 1, place), next_upper, before_upper),
         ])
-        left(up_inflow[chunk])
-        run(up_stash[chunk])
-        if chunk == 0:
-            arrive(mirror_stash)
-        run(own_grad[chunk] + own_stash[chunk])
         firsts += run(to_tokens(f_own, first_out, chunk, "within"))
 
     for step in range(half):
@@ -417,17 +439,15 @@
             Copy(fs_own, ms_own.at[inner], ms_own.at[behind], (section + 1, base + ahead), has_next, has_before),
             Copy(fs_low, ms_low.at[inner], ms_low.at[behind], (section + 1, base + ahead), next_upper, before_upper),
         ])
-    run(mirror_inflow)
+    for chunk in range(CHUNKS):
+        run(up_fresh[chunk] + own_fresh[chunk])
+    run(fresh_factors)
 
     backs = []
     for chunk in range(CHUNKS):
         if chunk == 0:
             arrive(stash_factors)
         arrive(up_stash[chunk], own_grad[chunk], own_stash[chunk])
-        left(up_stash[chunk])
-        run(up_fresh[chunk] + own_fresh[chunk])
-        if chunk == 0:
-            run(fresh_factors)
         backward(chunk)
         backs += run(to_tokens(dn_low, returned_low, chunk, "down") + to_tokens(dn_own, returned_own, chunk, "within"))
 
@@ -446,12 +466,7 @@
 
 def counts(half):
     remote = CHUNKS * (9 * half + 2) + 9 * half + 16
-    return remote, CHUNKS * 8 + 16
-
-
-def row_sums(tokens):
-    values = tokens.astype(f32)
-    return jnp.pad(jnp.sum(values * values, axis=-1, keepdims=True), ((0, 0), (0, LANES - 1)))
+    return remote, CHUNKS * 8 + 20
 
 
 def per_device(inflow, fresh, stash_held, grad_in, query_gain, key_gain, value_gain):
@@ -463,7 +478,6 @@
     gains_in = jnp.pad(
         jnp.concatenate([query_gain, key_gain, value_gain], axis=0), ((0, 5), (0, 0))
     )
-    fresh_sums = jnp.pad(row_sums(fresh)[None], ((0, half - 1), (0, 0), (0, 0)))
     tokens = jax.ShapeDtypeStruct((rows, features), bf16)
     any_space = pl.BlockSpec(memory_space=pl.ANY)
     wide = pltpu.VMEM((length, group), bf16)
@@ -472,7 +486,7 @@
     remote, local = counts(half)
     first_out, second_out, evicted, stash, returned_own, returned_low = pl.pallas_call(
         functools.partial(kernel, sections, tensors),
-        in_specs=[any_space] * 8,
+        in_specs=[any_space] * 5,
         out_specs=[any_space] * 6,
         out_shape=[tokens] * 6,
         scratch_shapes=[wide] * 12
@@ -480,27 +494,30 @@
         + [slots] * 2
         + [narrow] * 2
         + [pltpu.VMEM((8, group), f32)]
+        + [pltpu.VMEM((rows, features), bf16)] * 3
+        + [pltpu.VMEM((rows, LANES), f32)] * 2
+        + [pltpu.VMEM((half, rows, LANES), f32)]
         + [
             pltpu.SemaphoreType.DMA((remote,)),
             pltpu.SemaphoreType.DMA((remote,)),
             pltpu.SemaphoreType.DMA((local,)),
         ],
         compiler_params=pltpu.CompilerParams(
-            collective_id=0, has_side_effects=True, vmem_limit_bytes=54 * 1024 * 1024
+            collective_id=0, has_side_effects=True, vmem_limit_bytes=56 * 1024 * 1024
         ),
         cost_estimate=pl.CostEstimate(
             flops=length * length * group * 40,
             bytes_accessed=length * group * 40,
             transcendentals=length * length * group // 16,
         ),
-    )(inflow, fresh, held, grad, row_sums(inflow), fresh_sums, row_sums(held), gains_in)
+    )(inflow, fresh, held, grad, gains_in)
 
     received = lax.axis_index("tensor") < half
     returned = returned_own.astype(f32) + jnp.where(received, returned_low.astype(f32), 0.0)
     values = stash.astype(f32)
     factor = lax.rsqrt(jnp.mean(values * values, axis=-1, keepdims=True) + epsilon)
     scaled = values * factor
-    inner = jnp.mean(returned * scaled, axis=-1, keepdims=True)
+    inner = factor * jnp.mean(returned * values, axis=-1, keepdims=True)
     grad_out = (grad.astype(f32) + factor * (returned - scaled * inner)).astype(bf16)
     return (first_out[None], second_out[None], evicted[None], grad_out[None])
 

time: 485 us -> 436 us (0.90)
  Pallas kernels: 457 us -> 414 us
  other arithmetic: 15.9 us -> 10.9 us
    pallas_call x1, Pallas kernels: 457 us -> 414 us  [per_device(): pl.pallas_call(functools.partial(kernel, sections, tensors), in_specs=[an...]
    reduce_sum x4 -> x0, other arithmetic: 8.9 us -> none  [the longest x1 4.8 us: per_device(): inner = jnp.mean(returned * scaled, axis=-1, keepdims=True)]
where the time goes in v3:
time: 436 us; the launch traced here: 434 us
  Pallas kernels  414 us (95%)
  other arithmetic  10.9 us (2%)
  local copies, waits for them, and re-layouts  8.32 us (2%)
    pallas_call x1, Pallas kernels, per_device(): pl.pallas_call(functools.partial(kernel, sections, tensors), in_specs=[an...  414 us

profile of v3, /device:TPU:16, one launch (start us, length us, event | category | flops | bytes accessed | tf_op | source)
XLA Modules:
  0.0 434.2 jit_solution(17651916218943379709)
XLA Ops:
  0.6 1.4 select_maximum_fusion.gains_in
  2.1 0.0 copy-start.6
  2.1 414.3 %shard_map.102 = (bf16[128,12288]{1,0:T(8,128)(2,1)}, bf16[128,12288]{1,0:T(8,128)(2,1)}, bf16[128,12288]{1,0:T(8,128)(2,1)}, bf16[128,12288]{1,0:T(8,128)(2,1)}...) custom-call(bf16[128,12288]{1,0:T(8,128)(2,1)} %bitcast.13, bf16[128,12288]{1,0:T(8,128)(2,1)} %fresh.1, ...), custom_call_target="tpu_custom_call" | custom-call | flops 16106127360 | bytes 62914560 | tf_op jit(solution)/shard_map/pallas_call | solution.py:487
  416.4 0.0 copy-start
  416.4 0.0 copy-start.1
  416.4 0.0 copy-start.2
  416.4 5.8 %fusion = (f32[128]{0:T(128)S(1)}, f32[128]{0:T(128)S(1)}) fusion(bf16[128,12288]{1,0:T(8,128)(2,1)} %get-tuple-element.13, bf16[128,12288]{1,0:T(8,128)(2,1)} %get-tuple-element.15, pred[]{:T(512)S(6)} %lt.3, bf16[128,12288]{1,0:T(8,128)(2,1)} %get-tuple-element.14), kind=kLoop, calls=%fused_computation.3 | loop fusion | flops 14155520 | bytes 9438209 | tf_op jit(solution)/shard_map/reduce_sum | solution.py:518
  422.2 0.0 copy-done.6
  422.2 0.0 copy-done
  422.3 0.0 copy-done.1
  422.3 0.6 copy-done.2
  422.9 0.0 copy-start.5
  422.9 3.6 fusion.7
  426.5 0.0 copy-done.5
  426.5 0.0 copy-start.4
  426.5 1.7 copy.14
  428.1 1.4 copy-done.4
  429.5 0.0 copy-start.3
  429.5 1.7 copy.15
  431.1 1.4 copy-done.3
  432.5 1.7 copy.16
  (1 shorter events, 0.0 us)
Async XLA Ops:
  2.1 420.2 %copy-start.6 = (bf16[1,128,12288]{2,1,0:T(8,128)(2,1)S(1)}, bf16[1,128,12288]{2,1,0:T(8,128)(2,1)}, u32[]{:S(2)}) copy-start(bf16[1,128,12288]{2,1,0:T(8,128)(2,1)} %param.10) | copy-start | bytes 9437188
  416.4 5.9 %copy-start = (bf16[128,12288]{1,0:T(8,128)(2,1)S(1)}, bf16[128,12288]{1,0:T(8,128)(2,1)}, u32[]{:S(2)}) copy-start(bf16[128,12288]{1,0:T(8,128)(2,1)} %get-tuple-element.13) | copy-start | bytes 9437188
  416.4 5.9 %copy-start.1 = (bf16[128,12288]{1,0:T(8,128)(2,1)S(1)}, bf16[128,12288]{1,0:T(8,128)(2,1)}, u32[]{:S(2)}) copy-start(bf16[128,12288]{1,0:T(8,128)(2,1)} %get-tuple-element.14) | copy-start | bytes 9437188
  416.4 6.5 %copy-start.2 = (bf16[128,12288]{1,0:T(8,128)(2,1)S(1)}, bf16[128,12288]{1,0:T(8,128)(2,1)}, u32[]{:S(2)}) copy-start(bf16[128,12288]{1,0:T(8,128)(2,1)} %get-tuple-element.15) | copy-start | bytes 9437188
  422.9 3.6 copy-start.5
  426.5 3.0 copy-start.4
  429.5 3.0 copy-start.3
